TPU v7x, 128 devices: a whole 4x4x4 slice. The times are simulated.
128 devices in a mesh: row: 64 (over x, z, y), col: 2 (over core).
Axes of the slice: x: 4, y: 4, z: 4, core: 2. Of those that a mesh axis runs over, the one named last changes fastest.
Arguments:
- blocks: float32 [1024, 25, 128, 128], P('row'), may hold values from -1 to 1, as said below
- columns: int32 [1024, 25], P('row'), may hold values from 0 to 1023, as said below
- current: float32 [64, 131072], P('col', 'row'), may hold values from -90 to 90
- directions: float32 [64, 131072], P('col', 'row'), may hold values from -90 to 90
- ritz_values: float32 [64], P('col'), may hold values from -1.5 to 1.5
- rotation: float32 [192, 64], replicated, may hold values from -0.4375 to 0.4375
Outputs:
- next_current: float32 [64, 131072], P('col', 'row')
- next_directions: float32 [64, 131072], P('col', 'row')
- projected: float32 [64, 64], replicated
Inputs may be any that keep to these rules, and one draw needn't show every extreme that they name: Slot 0 of block row i holds column i. Its other slots hold distinct columns (i + d) mod 1024 with 1 <= d <= 32, and d = 32 occurs in every block row. `blocks`: slot 0 of every block row is a symmetric block.
All inputs are finite; a program needn't handle non-finite values.
Results may differ from a plain program's by a relative error of at most 0.0003.
Values sent between devices are 32-bit elements; how exact they have to be, the bound alone decides.
A program may use at most 128 MiB of HBM per device.

v0:
```python
import jax
import jax.numpy as jnp
from jax import lax
from jax.sharding import PartitionSpec as P

WB = 32


HIGH = lax.Precision.HIGHEST


def shifted(block, axis, distance):
    devices = range(lax.axis_size(axis))
    route = [((i - distance) % len(devices), i) for i in devices]
    return lax.ppermute(block, axis, route)


def on_device(blocks, columns, current, directions, ritz_values, rotation):
    rows_here = blocks.shape[0]
    width = blocks.shape[2]
    row_count = lax.axis_size("row")
    reach = (WB + rows_here - 1) // rows_here
    total_rows = rows_here * row_count
    length = rows_here * width
    first = lax.axis_index("row") * rows_here
    local = jnp.arange(rows_here, dtype=jnp.int32)
    offsets = jnp.mod(columns - (first + local)[:, None], total_rows)
    places = local[:, None] + offsets
    tail_places = places[:, 1:].reshape(-1)

    def apply_h(vectors):
        count = vectors.shape[0]
        pieces = [vectors]
        for step in range(1, reach + 1):
            pieces.append(shifted(vectors, "row", -step))
        window = jnp.concatenate(pieces, axis=1).reshape(count, (reach + 1) * rows_here, width)
        picked = window[:, places, :]
        direct = jnp.einsum("rsab,crsb->cra", blocks, picked, precision=HIGH)
        own = vectors.reshape(count, rows_here, width)
        back = jnp.einsum("rsab,cra->rscb", blocks[:, 1:], own, precision=HIGH).reshape(
            -1, count, width
        )
        landed = jax.ops.segment_sum(back, tail_places, num_segments=(reach + 1) * rows_here)
        parts = landed.reshape(reach + 1, rows_here, count, width)
        mine = parts[0]
        for step in range(1, reach + 1):
            mine = mine + shifted(parts[step], "row", step)
        return (direct + jnp.transpose(mine, (1, 0, 2))).reshape(count, length)

    half = current.shape[0]
    both = apply_h(jnp.concatenate([current, directions], axis=0))
    h_current = both[:half]
    h_directions = both[half:]
    resid = h_current - ritz_values[:, None] * current
    h_resid = apply_h(resid)
    basis = jnp.stack([current, resid, directions])
    image = jnp.stack([h_current, h_resid, h_directions])
    full_basis, full_image = (
        lax.all_gather(basis, "col", axis=1, tiled=True),
        lax.all_gather(image, "col", axis=1, tiled=True),
    )
    flat_basis = full_basis.reshape(-1, length)
    flat_image = full_image.reshape(-1, length)
    factor = 1.0 / (length * row_count)
    gram_part = jnp.dot(flat_basis, flat_basis.T, precision=HIGH) * factor
    kmat_part = jnp.dot(flat_basis, flat_image.T, precision=HIGH) * factor
    gram, kmat = lax.psum((gram_part, kmat_part), "row")
    small = jnp.dot(jnp.dot(rotation.T, gram, precision=HIGH), rotation, precision=HIGH)
    lower = jnp.linalg.cholesky(small)
    left = lax.linalg.triangular_solve(lower, rotation.T, left_side=True, lower=True)
    states = rotation.shape[1]
    mine_left = lax.dynamic_slice_in_dim(left, lax.axis_index("col") * half, half, 0)
    next_current = jnp.dot(mine_left, flat_basis, precision=HIGH)
    next_directions = jnp.dot(mine_left[:, states:], flat_basis[states:], precision=HIGH)
    projected = jnp.dot(jnp.dot(left, kmat, precision=HIGH), left.T, precision=HIGH)
    return (next_current, next_directions, projected)


def solution(mesh):
    in_specs = (
        P("row", None, None, None),
        P("row", None),
        P("col", "row"),
        P("col", "row"),
        P("col"),
        P(),
    )
    out_specs = (P("col", "row"), P("col", "row"), P())
    return jax.shard_map(
        on_device, mesh=mesh, in_specs=in_specs, out_specs=out_specs, check_vma=False
    )
```

profile of v0, /device:TPU:1, one launch (start us, length us, event | category | flops | bytes accessed | tf_op | source)
XLA Modules:
  0.0 417.1 jit_solution(15705287860899435616)
XLA Ops:
  9.2 9.3 %collective-permute-start = (f32[64,2048]{1,0:T(8,128)S(1)}, f32[64,2048]{1,0:T(8,128)S(1)}, u32[]{:S(2)}, u32[]{:S(2)}) collective-permute-start(f32[64,2048]{1,0:T(8,128)S(1)} %constant_dynamic-update-slice_fusion), channel_id=1, source_target_pairs={{2,0},{4,2},{6,4},{8,6},{10,8},{12,10},{14,12},{16,14},{18,16},{20... | collective-permute-start | bytes 1572872 | tf_op jit(solution)/shard_map/ppermute | solution.py:15
  19.9 19.2 %fusion.2 = f32[16,64,24,128]{3,1,2,0:T(8,128)} fusion(f32[16,25,128,128]{3,2,1,0:T(8,128)} %param.6, f32[64,16,128,1]{2,1,0,3:T(8,128)S(1)} %bitcast.95), kind=kOutput, calls=%fused_computation.6 | convolution fusion | flops 4831838208 | bytes 38273024 | tf_op jit(solution)/shard_map/rsab,cra->rscb/dot_general | solution.py:40
  39.2 39.5 %scatter_fusion = f32[48,64,128]{2,1,0:T(8,128)S(1)} fusion(f32[48,64,128]{2,1,0:T(8,128)S(1)} %broadcast_in_dim.16, s32[384]{0:T(512)S(1)} %reshape.90, f32[384,64,128]{2,1,0:T(8,128)} %bitcast.85), kind=kCustom, calls=%fused_computation.2 | custom fusion | flops 3145728 | bytes 37750272 | tf_op jit(solution)/shard_map/scatter-add | solution.py:43
  80.4 1.9 collective-permute-start.3
  83.3 1.5 copy_bitcast_fusion
  84.8 6.0 %gather_fusion = f32[400,64,128]{2,1,0:T(8,128)} fusion(f32[64,48,128]{2,0,1:T(8,128)S(1)} %copy_bitcast_fusion, s32[1024]{0:T(1024)S(1)} %pad_clamp_fusion), kind=kCustom, calls=%fused_computation | custom fusion | bytes 26216000 | tf_op jit(solution)/shard_map/gather | solution.py:37
  90.8 14.6 %collective-permute-done.2 = f32[16,64,128]{2,1,0:T(8,128)} collective-permute-done((f32[16,64,128]{2,1,0:T(8,128)}, f32[16,64,128]{2,1,0:T(8,128)}, u32[]{:S(2)}, u32[]{:S(2)}) %collective-permute-start.2) | collective-permute-done | bytes 524320 | tf_op jit(solution)/shard_map/ppermute | solution.py:15
  105.4 2.3 collective-permute-done.3
  107.7 32.3 %fusion.5 = f32[64,16,128]{2,0,1:T(8,128)S(1)} fusion(f32[64,16,25,128]{3,0,2,1:T(8,128)} %bitcast.84, f32[16,25,128,128]{3,2,1,0:T(8,128)} %param.6, f32[16,64,128]{2,1,0:T(8,128)} %collective-permute-done.3, f32[16,64,128]{2,1,0:T(8,128)} %collective-permute-done.2, f32[48,64,128]{2,1,0:T(8,128)S(1)} %scatter_fusion), kind=kOutput, calls=%fused_computation.12 | convolution fusion | flops 5033558016 | bytes 41418752 | tf_op jit(solution)/shard_map/rsab,crsb->cra/dot_general | solution.py:38
  140.2 6.4 %collective-permute-start.4 = (f32[32,2048]{1,0:T(8,128)S(1)}, f32[32,2048]{1,0:T(8,128)}, u32[]{:S(2)}, u32[]{:S(2)}) collective-permute-start(f32[32,2048]{1,0:T(8,128)S(1)} %bitcast_subtract_fusion), channel_id=1, source_target_pairs={{2,0},{4,2},{6,4},{8,6},{10,8},{12,10},{14,12},{16,14},{18,16},{20... | collective-permute-start | bytes 786440 | tf_op jit(solution)/shard_map/ppermute | solution.py:15
  146.6 17.3 %fusion = f32[16,32,24,128]{3,1,2,0:T(8,128)} fusion(f32[16,25,128,128]{3,2,1,0:T(8,128)} %param.6, f32[32,16,128,1]{2,1,0,3:T(8,128)S(1)} %bitcast.98), kind=kOutput, calls=%fused_computation.4 | convolution fusion | flops 2415919104 | bytes 31719424 | tf_op jit(solution)/shard_map/rsab,cra->rscb/dot_general | solution.py:40
  164.0 34.3 %scatter_fusion.1 = f32[48,32,128]{2,1,0:T(8,128)S(1)} fusion(f32[48,32,128]{2,1,0:T(8,128)S(1)} %broadcast_in_dim.17, s32[384]{0:T(512)S(1)} %reshape.90, f32[384,32,128]{2,1,0:T(8,128)} %bitcast.86), kind=kCustom, calls=%fused_computation.3 | custom fusion | flops 1572864 | bytes 18875904 | tf_op jit(solution)/shard_map/scatter-add | solution.py:43
  199.1 1.4 collective-permute-start.6
  200.5 3.6 collective-permute-start.7
  206.7 3.9 gather_fusion.1
  211.0 3.0 collective-permute-done.7
  214.0 30.8 %fusion.10 = f32[32,16,128]{2,0,1:T(8,128)S(1)} fusion(f32[16,32,128]{2,1,0:T(8,128)} %collective-permute-done.7, f32[16,32,128]{2,1,0:T(8,128)S(1)} %collective-permute-done.6, f32[48,32,128]{2,1,0:T(8,128)S(1)} %scatter_fusion.1, f32[32,16,25,128]{3,0,2,1:T(8,128)} %bitcast.90, f32[16,25,128,128]{3,2,1,0:T(8,128)} %param.6), kind=kOutput, calls=%fused_computation.27 | convolution fusion | flops 2516779008 | bytes 33816576 | tf_op jit(solution)/shard_map/rsab,crsb->cra/dot_general | solution.py:38
  246.4 4.1 convolution_multiply_fusion.1
  250.5 9.9 %all-gather.5.cloned.1.call-done = f32[3,64,2048]{2,1,0:T(8,128)} async-done(((f32[3,32,2048]{2,1,0:T(8,128)}), f32[3,64,2048]{2,1,0:T(8,128)}) %all-gather.5.cloned.1.call-update) | async-done | bytes 1572880 | tf_op jit(solution)/shard_map/all_gather | solution.py:60
  260.4 4.0 convolution_multiply_fusion
  264.6 127.1 %all-reduce.3.cloned.1.call-done = (f32[192,192]{1,0:T(8,128)}, f32[192,192]{1,0:T(8,128)}) async-done(((f32[192,192]{1,0:T(8,128)}, f32[192,192]{1,0:T(8,128)}), (f32[192,192]{1,0:T(8,128)}, f32[192,192]{1,0:T(8,128)})) %all-reduce.3.cloned.1.call-update) | async-done | bytes 294928 | tf_op jit(solution)/shard_map/psum | solution.py:67
  393.1 5.8 %cholesky.16 = f32[64,64]{1,0:T(8,128)S(1)} custom-call(f32[64,64]{1,0:T(8,128)S(1)} %fusion.15), custom_call_target="Cholesky" | custom-call | tf_op jit(solution)/shard_map/jit(cholesky)/cholesky | solution.py:69
  400.3 4.9 %custom-call.6 = f32[1,64,64]{1,2,0:T(8,128)S(1)} custom-call(f32[1,64,64]{2,1,0:T(8,128)S(1)} %fusion.12), custom_call_target="InvertDiagBlocksLowerTriangular" | custom-call | tf_op jit(solution)/shard_map/triangular_solve | solution.py:70
  407.5 1.7 fusion.16
  (66 shorter events, 18.3 us)
Async XLA Ops:
  7.2 384.5 %copy-start = (f32[192,64]{0,1:T(8,128)S(1)}, f32[192,64]{0,1:T(8,128)}, u32[]{:S(2)}) copy-start(f32[192,64]{0,1:T(8,128)} %param.11) | copy-start | bytes 147460
  7.2 239.2 %all-gather.3.cloned.1.call-start = ((), (), s32[]{:S(2)}) async-start(), calls=%async_computation | async-start | bytes 2359296 | tf_op jit(solution)/shard_map/all_gather | solution.py:59
  9.2 29.9 %copy-start.2 = (f32[64,2048]{1,0:T(8,128)}, f32[64,2048]{1,0:T(8,128)S(1)}, u32[]{:S(2)}) copy-start(f32[64,2048]{1,0:T(8,128)S(1)} %constant_dynamic-update-slice_fusion) | copy-start | bytes 1572868
  9.2 73.3 %collective-permute-start = (f32[64,2048]{1,0:T(8,128)S(1)}, f32[64,2048]{1,0:T(8,128)S(1)}, u32[]{:S(2)}, u32[]{:S(2)}) collective-permute-start(f32[64,2048]{1,0:T(8,128)S(1)} %constant_dynamic-update-slice_fusion), channel_id=1, source_target_pairs={{2,0},{4,2},{6,4},{8,6},{10,8},{12,10},{14,12},{16,14},{18,16},{20... | collective-permute-start | bytes 1572872 | tf_op jit(solution)/shard_map/ppermute | solution.py:15
  18.5 64.8 %collective-permute-start.1 = (f32[64,2048]{1,0:T(8,128)S(1)}, f32[64,2048]{1,0:T(8,128)}, u32[]{:S(2)}, u32[]{:S(2)}) collective-permute-start(f32[64,2048]{1,0:T(8,128)S(1)} %constant_dynamic-update-slice_fusion), channel_id=1, source_target_pairs={{4,0},{6,2},{8,4},{10,6},{12,8},{14,10},{16,12},{18,14},{20,16},{2... | collective-permute-start | bytes 1572872 | tf_op jit(solution)/shard_map/ppermute | solution.py:15
  79.7 25.6 %collective-permute-start.2 = (f32[16,64,128]{2,1,0:T(8,128)}, f32[16,64,128]{2,1,0:T(8,128)}, u32[]{:S(2)}, u32[]{:S(2)}) collective-permute-start(f32[16,64,128]{2,1,0:T(8,128)} %get-tuple-element.7), channel_id=1, source_target_pairs={{126,0},{0,2},{2,4},{4,6},{6,8},{8,10},{10,12},{12,14},{14,16},{16... | collective-permute-start | bytes 1572872 | tf_op jit(solution)/shard_map/ppermute | solution.py:15
  80.4 27.3 %collective-permute-start.3 = (f32[16,64,128]{2,1,0:T(8,128)}, f32[16,64,128]{2,1,0:T(8,128)}, u32[]{:S(2)}, u32[]{:S(2)}) collective-permute-start(f32[16,64,128]{2,1,0:T(8,128)} %get-tuple-element.8), channel_id=1, source_target_pairs={{124,0},{126,2},{0,4},{2,6},{4,8},{6,10},{8,12},{10,14},{12,16},{1... | collective-permute-start | bytes 1572872 | tf_op jit(solution)/shard_map/ppermute | solution.py:15
  82.5 0.8 copy-start.5
  107.7 32.4 %copy-start.3 = (f32[32,2048]{1,0:T(8,128)S(1)}, f32[32,2048]{1,0:T(8,128)}, u32[]{:S(2)}) copy-start(f32[32,2048]{1,0:T(8,128)} %param.8) | copy-start | bytes 786436
  107.7 32.4 %copy-start.6 = (f32[32]{0:T(128)S(1)}, f32[32]{0:T(128)}, u32[]{:S(2)}) copy-start(f32[32]{0:T(128)} %param.10) | copy-start | bytes 388
  140.2 65.4 %collective-permute-start.4 = (f32[32,2048]{1,0:T(8,128)S(1)}, f32[32,2048]{1,0:T(8,128)}, u32[]{:S(2)}, u32[]{:S(2)}) collective-permute-start(f32[32,2048]{1,0:T(8,128)S(1)} %bitcast_subtract_fusion), channel_id=1, source_target_pairs={{2,0},{4,2},{6,4},{8,6},{10,8},{12,10},{14,12},{16,14},{18,16},{20... | collective-permute-start | bytes 786440 | tf_op jit(solution)/shard_map/ppermute | solution.py:15
  146.6 59.0 %collective-permute-start.5 = (f32[32,2048]{1,0:T(8,128)S(1)}, f32[32,2048]{1,0:T(8,128)}, u32[]{:S(2)}, u32[]{:S(2)}) collective-permute-start(f32[32,2048]{1,0:T(8,128)S(1)} %bitcast_subtract_fusion), channel_id=1, source_target_pairs={{4,0},{6,2},{8,4},{10,6},{12,8},{14,10},{16,12},{18,14},{20,16},{2... | collective-permute-start | bytes 786440 | tf_op jit(solution)/shard_map/ppermute | solution.py:15
  164.0 40.5 %copy-start.4 = (f32[32,2048]{1,0:T(8,128)S(1)}, f32[32,2048]{1,0:T(8,128)}, u32[]{:S(2)}) copy-start(f32[32,2048]{1,0:T(8,128)} %param.9) | copy-start | bytes 786436
  199.1 11.9 %collective-permute-start.6 = (f32[16,32,128]{2,1,0:T(8,128)}, f32[16,32,128]{2,1,0:T(8,128)S(1)}, u32[]{:S(2)}, u32[]{:S(2)}) collective-permute-start(f32[16,32,128]{2,1,0:T(8,128)} %get-tuple-element.9), channel_id=1, source_target_pairs={{126,0},{0,2},{2,4},{4,6},{6,8},{8,10},{10,12},{12,14},{14,16},{16... | collective-permute-start | bytes 786440 | tf_op jit(solution)/shard_map/ppermute | solution.py:15
  200.5 13.5 %collective-permute-start.7 = (f32[16,32,128]{2,1,0:T(8,128)}, f32[16,32,128]{2,1,0:T(8,128)}, u32[]{:S(2)}, u32[]{:S(2)}) collective-permute-start(f32[16,32,128]{2,1,0:T(8,128)} %get-tuple-element.10), channel_id=1, source_target_pairs={{124,0},{126,2},{0,4},{2,6},{4,8},{6,10},{8,12},{10,14},{12,16},{1... | collective-permute-start | bytes 786440 | tf_op jit(solution)/shard_map/ppermute | solution.py:15
  205.5 54.9 %all-gather.5.cloned.1.call-start = ((), (), s32[]{:S(2)}) async-start(), calls=%async_computation.1 | async-start | bytes 2359296 | tf_op jit(solution)/shard_map/all_gather | solution.py:60
  246.0 145.6 %all-reduce.3.cloned.1.call-start = ((), (), s32[]{:S(2)}) async-start(), calls=%async_computation.2 | async-start | bytes 786432 | tf_op jit(solution)/shard_map/psum | solution.py:67
  246.4 18.1 %copy-start.1 = (f32[3,64,2048]{2,1,0:T(8,128)S(1)}, f32[3,64,2048]{2,1,0:T(8,128)}, u32[]{:S(2)}) copy-start(f32[3,64,2048]{2,1,0:T(8,128)} %all-gather.3.cloned.1.call-done) | copy-start | bytes 4718596
Sparse Core Ops, SparseCore 0:
  205.6 14.7 all-gather.2
  246.2 14.2 all-gather.4
  265.7 125.8 all-reduce.2
where the time goes:
time: 421 us; the launch traced here: 417 us
  waiting for transfers between devices  157 us (37%)
  matrix products  114 us (27%)
  other arithmetic  91.3 us (22%)
  starting transfers between devices  24 us (6%)
  local copies, waits for them, and re-layouts  15.9 us (4%)
  between operations  14.1 us (3%)
    psum x1, waiting for transfers between devices, on_device(): gram, kmat = lax.psum((gram_part, kmat_part), 'row')  127 us
    scatter-add x2, other arithmetic, apply_h(): jax.ops.segment_sum(back, tail_places, num_segments=(reach + 1) * rows_here)  73.7 us
    dot_general x2, matrix products, apply_h(): direct = jnp.einsum('rsab,crsb->cra', blocks, picked, precision=HIGH)  63.1 us
    dot_general x2, matrix products, apply_h(): jnp.einsum('rsab,cra->rscb', blocks[:, 1:], own, precision=HIGH)  36.4 us
    ppermute x8, starting transfers between devices, shifted(): return lax.ppermute(block, axis, route)  23.6 us
    ppermute x8, waiting for transfers between devices, shifted(): return lax.ppermute(block, axis, route)  20.4 us
    all_gather x1, waiting for transfers between devices, on_device(): lax.all_gather(image, 'col', axis=1, tiled=True)  9.94 us
    gather x2, local copies, waits for them, and re-layouts, apply_h(): picked = window[:, places, :]  9.83 us
  transfers between devices with their start and end apart: 11, of which 6 were waited for; matrix products, arithmetic and copies ran while one was open for 39% of the time, Pallas kernels for 0%

commit v1 on v0

v1 whole, which is shorter than its diff:
```python
import functools

import jax
import jax.numpy as jnp
from jax import lax
from jax.experimental import pallas as pl
from jax.experimental.pallas import tpu as pltpu
from jax.sharding import PartitionSpec as P

WB = 32
F32 = jnp.float32
BF16 = jnp.bfloat16
MESH = pl.DeviceIdType.MESH
NN = (((1,), (0,)), ((), ()))
NT = (((1,), (1,)), ((), ()))
TN = (((0,), (0,)), ((), ()))
HIGH = lax.Precision.HIGHEST

RB = 8
W = 128
L = RB * W
SLABS = WB // RB + 1
CH = 256


def mm(a, b, dims):
    return lax.dot_general(a, b, dims, preferred_element_type=F32)


def mm_high(a, b, dims):
    return lax.dot_general(a, b, dims, precision=HIGH, preferred_element_type=F32)


def split(v):
    hi = v.astype(BF16)
    return hi, (v - hi.astype(F32)).astype(BF16)


def inverse_factor(g):
    n = g.shape[0]
    rows = lax.broadcasted_iota(jnp.int32, (n, 2 * n), 0)
    lanes = lax.broadcasted_iota(jnp.int32, (n, 2 * n), 1)
    eye = jnp.where(rows + n == lanes, 1.0, 0.0).astype(F32)
    a = jnp.concatenate([g, jnp.zeros((n, n), F32)], axis=1) + eye

    def step(k, a):
        row = jnp.sum(jnp.where(rows == k, a, 0.0), axis=0, keepdims=True)
        col = jnp.sum(jnp.where(lanes == k, a, 0.0), axis=1, keepdims=True)
        pivot = jnp.sum(jnp.where(lanes[:1] == k, row, 0.0), axis=1, keepdims=True)
        factor = jnp.where(rows[:, :1] > k, col / pivot, 0.0)
        return a - factor * row

    a = lax.fori_loop(0, n, step, a)
    diag = jnp.sum(jnp.where(rows == lanes, a, 0.0), axis=1, keepdims=True)
    return a[:, n:] * (1.0 / jnp.sqrt(diag))


def kernel(dims, ntot, inv_ref, blocks, current, directions, ritz, rot, nc, nd, proj, *scratch):
    stages = scratch[:RB]
    (mh, ml, xw, xx, zw, zz, pbuf, inbuf, tb, hx, pv, lam, ostage, arbuf,
     blk_sem, loc_sem, exs, exr, xs, xr, zs, zr, bs, br, ars, arr, outs, outr) = scratch[RB:]
    half, full = current.shape
    slots = blocks.shape[1]
    rows_n = 1
    for m in dims:
        rows_n *= m
    units = 2 * rows_n
    r = lax.axis_index("row")
    h = lax.axis_index("col")
    u = 2 * r + h
    down = lax.rem(u + units - 1, units)
    up = lax.rem(u + 1, units)
    down_id = (down // 2, lax.rem(down, 2))
    up_id = (up // 2, lax.rem(up, 2))
    sib = (r, 1 - h)

    groups = [(2, h, lambda c: (r, c))]
    stride = 1
    for m in reversed(dims):
        c = lax.rem(r // stride, m)
        groups.append((m, c, functools.partial(lambda c, stride, k: (r + (k - c) * stride, h), c, stride)))
        stride *= m

    for i in range(RB):
        pltpu.make_async_copy(
            blocks.at[h * RB + i], stages[i].at[pl.ds(0, slots)], blk_sem.at[i]
        ).start()
    mine = pl.multiple_of(h * L, L)
    other = pl.multiple_of((1 - h) * L, L)
    hrows = pl.multiple_of(h * half, half)
    loc_x = pltpu.make_async_copy(current.at[:, pl.ds(mine, L)], xw.at[0, pl.ds(hrows, half)], loc_sem.at[0])
    loc_x.start()
    loc_p = pltpu.make_async_copy(directions.at[:, pl.ds(mine, L)], pv.at[pl.ds(hrows, half)], loc_sem.at[1])
    loc_p.start()

    barrier = pltpu.get_barrier_semaphore()
    partners = [down_id, up_id]
    for m, c, member in groups:
        for k in range(1, m):
            partners.append(member(lax.rem(c + k, m)))
    for d in partners:
        pl.semaphore_signal(barrier, inc=1, device_id=d, device_id_type=MESH)

    er = lax.broadcasted_iota(jnp.int32, (half, half), 0) == lax.broadcasted_iota(jnp.int32, (half, half), 1)
    lam_own = jnp.sum(jnp.where(er, jnp.broadcast_to(ritz[...], (half, half)), 0.0), axis=1, keepdims=True)
    lam[pl.ds(hrows, half), :] = jnp.broadcast_to(lam_own, (half, W))
    for i in range(RB):
        stages[i][slots] = jnp.zeros((W, W), F32)
    zero = jnp.zeros((W, W), BF16)
    for j in range(0, RB, 2):
        for m_ref in (mh, ml):
            m_ref[(j + 1) * W:(j + 2) * W, j * W:(j + 1) * W] = zero
            m_ref[j * W:(j + 1) * W, (WB + j + 1) * W:(WB + j + 2) * W] = zero
    pl.semaphore_wait(barrier, len(partners))

    def remote(src, dst, ssem, rsem, dev):
        return pltpu.make_async_remote_copy(
            src_ref=src, dst_ref=dst, send_sem=ssem, recv_sem=rsem, device_id=dev, device_id_type=MESH)

    ex = [
        remote(current.at[:, pl.ds(other, L)], xw.at[0, pl.ds(hrows, half)], exs.at[0], exr.at[0], sib),
        remote(directions.at[:, pl.ds(other, L)], pv.at[pl.ds(hrows, half)], exs.at[1], exr.at[1], sib),
        remote(lam.at[pl.ds(hrows, half)], lam.at[pl.ds(hrows, half)], exs.at[2], exr.at[2], sib),
    ]
    for c in ex:
        c.start()
    xcopy = [remote(xw.at[t], xw.at[t + 1], xs.at[t], xr.at[t], down_id) for t in range(SLABS - 1)]
    zcopy = [remote(zw.at[t], zw.at[t + 1], zs.at[t], zr.at[t], down_id) for t in range(SLABS - 1)]
    bcopy = [remote(pbuf.at[t], inbuf.at[t], bs.at[t], br.at[t], up_id) for t in range(SLABS - 1)]

    def to_parts(t):
        hi, lo = split(xw[t])
        xx[t, :2 * half] = hi
        xx[t, 2 * half:] = lo

    def expand(i):
        pltpu.make_async_copy(
            blocks.at[h * RB + i], stages[i].at[pl.ds(0, slots)], blk_sem.at[i]
        ).wait()
        hi, lo = split(stages[i][0] * 0.5)
        mh[i * W:(i + 1) * W, i * W:(i + 1) * W] = hi
        ml[i * W:(i + 1) * W, i * W:(i + 1) * W] = lo

        def one(d, carry):
            hi, lo = split(stages[i][inv_ref[h * RB + i, d]])
            at = pl.multiple_of((i + d) * W, W)
            mh[i * W:(i + 1) * W, pl.ds(at, W)] = hi
            ml[i * W:(i + 1) * W, pl.ds(at, W)] = lo
            return carry

        lax.fori_loop(1, WB + 1, one, 0, unroll=4)

    def times_m(src, t, write):
        def chunk(j, lo, hi):
            at = pl.multiple_of(t * L + j * CH, CH)
            a = mm(src[:, lo:hi], mh[lo:hi, pl.ds(at, CH)], NN)
            b = mm(src[:2 * half, lo:hi], ml[lo:hi, pl.ds(at, CH)], NN)
            write(pl.ds(pl.multiple_of(j * CH, CH), CH), a[:2 * half] + a[2 * half:] + b)

        if t == 0 or t == SLABS - 1:
            for j in range(L // CH):
                chunk(j, *((0, (j + 1) * CH) if t == 0 else (j * CH, L)))
        else:
            def body(j, carry):
                chunk(j, 0, L)
                return carry
            lax.fori_loop(0, L // CH, body, 0)

    def times_mt(t):
        def chunk(j, lo, hi):
            at = pl.ds(pl.multiple_of(j * CH, CH), CH)
            a = mm(xx[t, :, lo:hi], mh[at, t * L + lo:t * L + hi], NT)
            b = mm(xx[t, :2 * half, lo:hi], ml[at, t * L + lo:t * L + hi], NT)
            hx[:, at] += a[:2 * half] + a[2 * half:] + b

        if t == 0 or t == SLABS - 1:
            for j in range(L // CH):
                chunk(j, *((j * CH, L) if t == 0 else (0, (j + 1) * CH)))
        else:
            def body(j, carry):
                chunk(j, 0, L)
                return carry
            lax.fori_loop(0, L // CH, body, 0)

    def back(t):
        s = SLABS - 1 - t
        def put(at, v):
            pbuf[s, :, at] = v
        times_m(xx.at[0], t, put)
        if s > 0:
            bcopy[s - 1].wait_recv()
            pbuf[s] += inbuf[s - 1]
        bcopy[s].start()

    loc_x.wait()
    ex[0].wait()
    xcopy[0].start()
    to_parts(0)
    for i in range(RB):
        expand(i)
        if i == RB // 2:
            xcopy[0].wait_recv()
            xcopy[1].start()
    back(4)
    xcopy[1].wait_recv()
    xcopy[2].start()
    back(3)
    xcopy[2].wait_recv()
    xcopy[3].start()
    back(2)
    back(1)

    def put_hx(at, v):
        hx[:, at] = v
    times_m(xx.at[0], 0, put_hx)
    times_mt(0)
    for t in range(1, SLABS):
        if t == SLABS - 1:
            xcopy[t - 1].wait_recv()
        to_parts(t)
        times_mt(t)
    loc_p.wait()
    ex[1].wait()
    ex[2].wait()
    bcopy[SLABS - 2].wait_recv()

    rot_x = rot[:2 * half]
    rot_r = rot[2 * half:4 * half]
    rot_p = rot[4 * half:]
    for j in range(L // CH):
        at = slice(j * CH, (j + 1) * CH)
        x = xw[0, :, at]
        res = hx[:, at] + inbuf[SLABS - 2, :, at] - jnp.concatenate([lam[...]] * (CH // W), axis=1) * x
        zp = mm_high(rot_r, res, TN) + mm_high(rot_p, pv[:, at], TN)
        z = zp + mm_high(rot_x, x, TN)
        ostage[1, :, at] = zp
        zw[0, :, at] = z
        hi, lo = split(z)
        zz[:2 * half, at] = hi
        zz[2 * half:, at] = lo
    zcopy[0].start()

    def sum_start(which, g, value):
        m, c, member = groups[g]
        buf = arbuf.at[which, g]
        buf[c] = value
        for k in range(1, m):
            remote(buf.at[c], buf.at[c], ars.at[which, g, k - 1], arr.at[which, g, k - 1],
                   member(lax.rem(c + k, m))).start()

    def sum_finish(which, g):
        m, c, member = groups[g]
        buf = arbuf.at[which, g]
        for k in range(1, m):
            remote(buf.at[c], buf.at[c], ars.at[which, g, k - 1], arr.at[which, g, k - 1],
                   member(lax.rem(c + k, m))).wait()
        total = buf[0]
        for k in range(1, m):
            total = total + buf[k]
        return total

    def z_times_m(t):
        def put(at, v):
            tb[t, :, at] = v
        times_m(zz, t, put)

    def z_next(t):
        zcopy[t].wait_recv()
        if t + 1 < SLABS - 1:
            zcopy[t + 1].start()

    def s_part(t):
        return mm_high(tb[t], zw[t], NT)

    def fold(v):
        return jnp.concatenate([v[:half], v[half:]], axis=1)

    def unfold(v):
        return jnp.concatenate([v[:, :2 * half], v[:, 2 * half:]], axis=0)

    sum_start(0, 0, fold(mm_high(zw[0], zw[0], NT)))
    z_times_m(0)
    sum_start(0, 1, sum_finish(0, 0))
    z_next(0)
    z_times_m(1)
    sum_start(0, 2, sum_finish(0, 1))
    z_next(1)
    z_times_m(2)
    sum_start(0, 3, sum_finish(0, 2))
    z_times_m(3)
    z_next(2)
    small = unfold(sum_finish(0, 3)) * (1.0 / ntot)
    li = inverse_factor(small)
    z_times_m(4)
    for j in range(L // CH):
        at = slice(j * CH, (j + 1) * CH)
        ostage[0, :, at] = mm_high(li, zw[0, :, at], NN)
        ostage[1, :, at] = mm_high(li, ostage[1, :, at], NN)
    orows = pl.multiple_of((1 - h) * half, half)
    ocopy = []
    for k, out in enumerate((nc, nd)):
        ocopy.append(remote(ostage.at[k, pl.ds(orows, half)], out.at[:, pl.ds(mine, L)], outs.at[k], outr.at[k], sib))
        ocopy.append(pltpu.make_async_copy(ostage.at[k, pl.ds(hrows, half)], out.at[:, pl.ds(mine, L)], loc_sem.at[2 + k]))
    for c in ocopy:
        c.start()
    s = s_part(0)
    for t in range(1, SLABS - 1):
        s = s + s_part(t)
    z_next(SLABS - 2)
    s = s + s_part(SLABS - 1)
    sum_start(1, 0, fold(s))
    for g in range(1, len(groups)):
        sum_start(1, g, sum_finish(1, g - 1))
    s = unfold(sum_finish(1, len(groups) - 1)) * (1.0 / ntot)
    sym = s + jnp.transpose(s)
    proj[...] = mm_high(mm_high(li, sym, NN), li, NT)
    for c in ocopy:
        c.wait()
    for c in xcopy + zcopy + bcopy:
        c.wait_send()


def on_device(dims, ntot, blocks, columns, current, directions, ritz_values, rotation):
    rows_here, slots = columns.shape
    half, length = current.shape
    states = rotation.shape[1]
    total_rows = ntot // W
    rows = lax.axis_index("row") * rows_here + jnp.arange(rows_here, dtype=jnp.int32)
    offsets = jnp.mod(columns - rows[:, None], total_rows)
    hit = offsets[:, None, :] == jnp.arange(WB + 1, dtype=jnp.int32)[None, :, None]
    inv = slots + jnp.sum(jnp.where(hit, jnp.arange(slots, dtype=jnp.int32) - slots, 0), axis=2)

    any_ = pl.BlockSpec(memory_space=pl.ANY)
    vmem = pl.BlockSpec(memory_space=pltpu.VMEM)
    smem = pl.BlockSpec(memory_space=pltpu.SMEM)
    n_groups = 1 + len(dims)
    most = max((2,) + tuple(dims))
    dma = pltpu.SemaphoreType.DMA
    hops = SLABS - 1
    scratch = [pltpu.VMEM((slots + 1, W, W), F32) for _ in range(RB)] + [
        pltpu.VMEM((L, SLABS * L), BF16),
        pltpu.VMEM((L, SLABS * L), BF16),
        pltpu.VMEM((SLABS, states, L), F32),
        pltpu.VMEM((SLABS, 2 * states, L), BF16),
        pltpu.VMEM((SLABS, states, L), F32),
        pltpu.VMEM((2 * states, L), BF16),
        pltpu.VMEM((hops, states, L), F32),
        pltpu.VMEM((hops, states, L), F32),
        pltpu.VMEM((SLABS, states, L), F32),
        pltpu.VMEM((states, L), F32),
        pltpu.VMEM((states, L), F32),
        pltpu.VMEM((states, W), F32),
        pltpu.VMEM((2, states, L), F32),
        pltpu.VMEM((2, n_groups, most, half, 2 * states), F32),
        dma((RB,)), dma((4,)), dma((3,)), dma((3,)),
        dma((hops,)), dma((hops,)), dma((hops,)), dma((hops,)), dma((hops,)), dma((hops,)),
        dma((2, n_groups, most)), dma((2, n_groups, most)), dma((2,)), dma((2,)),
    ]
    return pl.pallas_call(
        functools.partial(kernel, dims, ntot),
        out_shape=(
            jax.ShapeDtypeStruct((half, length), F32),
            jax.ShapeDtypeStruct((half, length), F32),
            jax.ShapeDtypeStruct((states, states), F32),
        ),
        in_specs=[smem, any_, any_, any_, vmem, vmem],
        out_specs=(any_, any_, vmem),
        scratch_shapes=scratch,
        compiler_params=pltpu.CompilerParams(
            collective_id=0, has_side_effects=True, vmem_limit_bytes=58 * 2**20
        ),
        name="lobpcg",
    )(inv, blocks, current, directions, ritz_values.reshape(1, half), rotation)


def solution(mesh):
    rows_n = mesh.shape["row"]
    side = round(rows_n ** (1 / 3))
    dims = (side, side, rows_n // (side * side))
    in_specs = (
        P("row", None, None, None),
        P("row", None),
        P("col", "row"),
        P("col", "row"),
        P("col"),
        P(),
    )
    out_specs = (P("col", "row"), P("col", "row"), P())
    ntot = rows_n * 2 * L
    return jax.shard_map(
        functools.partial(on_device, dims, ntot), mesh=mesh, in_specs=in_specs, out_specs=out_specs, check_vma=False
    )
```

time: 421 us -> 91.1 us (0.22)
  waiting for transfers between devices: 157 us -> 0 us
  matrix products: 114 us -> 0 us
  other arithmetic: 91.3 us -> 1.54 us
  Pallas kernels: 0 us -> 81.1 us
  starting transfers between devices: 24 us -> 0 us
  between operations: 14.1 us -> 0.66 us
  local copies, waits for them, and re-layouts: 15.9 us -> 6.38 us
    psum x1 -> x0, waiting for transfers between devices: 127 us -> none  [on_device(): gram, kmat = lax.psum((gram_part, kmat_part), 'row')]
    dot_general x12 -> x0, matrix products: 114 us -> none  [the longest x2 63.1 us: apply_h(): direct = jnp.einsum('rsab,crsb->cra', blocks, picked, precision=HIGH)]
    pallas_call x0 -> x1, Pallas kernels: none -> 81.1 us  [on_device(): pl.pallas_call(functools.partial(kernel, dims, ntot), out_shape=(jax.Shap...]
    scatter-add x2 -> x0, other arithmetic: 73.7 us -> none  [apply_h(): jax.ops.segment_sum(back, tail_places, num_segments=(reach + 1) * rows_here)]
    ppermute x8 -> x0, starting transfers between devices: 23.6 us -> none  [shifted(): return lax.ppermute(block, axis, route)]
    ppermute x8 -> x0, waiting for transfers between devices: 20.4 us -> none  [shifted(): return lax.ppermute(block, axis, route)]
    another operation x7 -> x0, other arithmetic: 14 us -> none  [the longest x3 6.52 us: on_device(): lower = jnp.linalg.cholesky(small)]
    all_gather x2 -> x0, waiting for transfers between devices: 9.96 us -> none  [the longest x1 9.94 us: on_device(): lax.all_gather(image, 'col', axis=1, tiled=True)]
  transfers between devices with their start and end apart: 11 -> 0, of which waited for: 6 -> 0; matrix products, arithmetic and copies ran while one was open for 39% -> 0% of each run, Pallas kernels for 0% -> 0%
where the time goes in v1:
time: 91.1 us; the launch traced here: 89.7 us
  Pallas kernels  81.1 us (89%)
  local copies, waits for them, and re-layouts  6.38 us (7%)
  other arithmetic  1.54 us (2%)
    pallas_call x1, Pallas kernels, on_device(): pl.pallas_call(functools.partial(kernel, dims, ntot), out_shape=(jax.Shap...  81.1 us
    unnamed x4, local copies, waits for them, and re-layouts  6.29 us

profile of v1, /device:TPU:1, one launch (start us, length us, event | category | flops | bytes accessed | tf_op | source)
XLA Modules:
  0.0 89.7 jit_solution(17964203290518005578)
XLA Ops:
  0.7 0.8 add_select_fusion
  1.4 0.1 copy.10
  1.5 0.1 select_reduce_fusion
  1.7 0.6 broadcast_add_fusion.inv_ref
  2.3 1.6 %copy.11.rot = f32[192,64]{1,0:T(8,128)} copy(f32[192,64]{0,1:T(8,128)} %param.11) | data formatting | bytes 98304 | tf_op args[5]
  3.9 81.1 %lobpcg.1 = (f32[32,2048]{1,0:T(8,128)}, f32[32,2048]{1,0:T(8,128)}, f32[64,64]{1,0:T(8,128)}) custom-call(s32[16,33]{1,0:T(8,128)} %broadcast_add_fusion.inv_ref, f32[16,25,128,128]{3,2,1,0:T(8,128)} %blocks.1, f32[32,2048]{1,0:T(8,128)} %current.1, f32[32,2048]{1,0:T(8,128)} %directions.1, f32[1,32]{1,0:T(1,128)} %bitcast.1, f32[192,64]{1,0:T(8,128)} %copy.11.rot), custom_call_target="tpu_custom_call" | custom-call | tf_op jit(solution)/shard_map/lobpcg/pallas_call | solution.py:359
  85.0 1.7 %copy.15 = f32[32,2048]{1,0:T(8,128)} copy(f32[32,2048]{1,0:T(8,128)} %get-tuple-element.6) | data formatting | bytes 524288
  86.7 1.7 %copy.16 = f32[32,2048]{1,0:T(8,128)} copy(f32[32,2048]{1,0:T(8,128)} %get-tuple-element.7) | data formatting | bytes 524288
  88.3 1.4 %copy.17 = f32[64,64]{1,0:T(8,128)} copy(f32[64,64]{1,0:T(8,128)} %get-tuple-element.8) | data formatting | bytes 32768
  (2 shorter events, 0.0 us)

commit v2 on v1

--- a/solution.py
+++ b/solution.py
@@ -57,8 +57,8 @@
 
 def kernel(dims, ntot, inv_ref, blocks, current, directions, ritz, rot, nc, nd, proj, *scratch):
     stages = scratch[:RB]
-    (mh, ml, xw, xx, zw, zz, pbuf, inbuf, tb, hx, pv, lam, ostage, arbuf,
-     blk_sem, loc_sem, exs, exr, xs, xr, zs, zr, bs, br, ars, arr, outs, outr) = scratch[RB:]
+    (mh, ml, xw, xx, zw, zz, zzp, pbuf, inbuf, tb, tin, hx, pv, lam, rotv, ritzv, ostage, bufa, bufb,
+     blk_sem, loc_sem, exs, exr, xs, xr, zs, zr, ts, tr, bs, br, asa, ara, asb, arb, outs, outr) = scratch[RB:]
     half, full = current.shape
     slots = blocks.shape[1]
     rows_n = 1
@@ -74,12 +74,16 @@
     up_id = (up // 2, lax.rem(up, 2))
     sib = (r, 1 - h)
 
-    groups = [(2, h, lambda c: (r, c))]
-    stride = 1
-    for m in reversed(dims):
-        c = lax.rem(r // stride, m)
-        groups.append((m, c, functools.partial(lambda c, stride, k: (r + (k - c) * stride, h), c, stride)))
-        stride *= m
+    ny = dims[-1]
+    nb = rows_n // ny
+    y = lax.rem(r, ny)
+    groups = [
+        (2 * ny, 2 * y + h, lambda k: (r - y + k // 2, lax.rem(k, 2)), (bufa, asa, ara)),
+        (nb, r // ny, lambda k: (k * ny + y, h), (bufb, asb, arb)),
+    ]
+
+    def row_at(k):
+        return (lax.rem(r + k + rows_n, rows_n), h)
 
     for i in range(RB):
         pltpu.make_async_copy(
@@ -92,17 +96,22 @@
     loc_x.start()
     loc_p = pltpu.make_async_copy(directions.at[:, pl.ds(mine, L)], pv.at[pl.ds(hrows, half)], loc_sem.at[1])
     loc_p.start()
+    loc_rot = pltpu.make_async_copy(rot, rotv, loc_sem.at[4])
+    loc_rot.start()
+    loc_ritz = pltpu.make_async_copy(ritz, ritzv, loc_sem.at[5])
+    loc_ritz.start()
 
     barrier = pltpu.get_barrier_semaphore()
-    partners = [down_id, up_id]
-    for m, c, member in groups:
+    partners = [down_id, up_id] + [row_at(k) for k in (-2, -1, 1, 2)]
+    for m, c, member, _ in groups:
         for k in range(1, m):
             partners.append(member(lax.rem(c + k, m)))
     for d in partners:
         pl.semaphore_signal(barrier, inc=1, device_id=d, device_id_type=MESH)
 
     er = lax.broadcasted_iota(jnp.int32, (half, half), 0) == lax.broadcasted_iota(jnp.int32, (half, half), 1)
-    lam_own = jnp.sum(jnp.where(er, jnp.broadcast_to(ritz[...], (half, half)), 0.0), axis=1, keepdims=True)
+    loc_ritz.wait()
+    lam_own = jnp.sum(jnp.where(er, jnp.broadcast_to(ritzv[...], (half, half)), 0.0), axis=1, keepdims=True)
     lam[pl.ds(hrows, half), :] = jnp.broadcast_to(lam_own, (half, W))
     for i in range(RB):
         stages[i][slots] = jnp.zeros((W, W), F32)
@@ -125,7 +134,8 @@
     for c in ex:
         c.start()
     xcopy = [remote(xw.at[t], xw.at[t + 1], xs.at[t], xr.at[t], down_id) for t in range(SLABS - 1)]
-    zcopy = [remote(zw.at[t], zw.at[t + 1], zs.at[t], zr.at[t], down_id) for t in range(SLABS - 1)]
+    zcopy = [remote(zw.at[0], zw.at[k], zs.at[k - 1], zr.at[k - 1], row_at(-k)) for k in (1, 2)]
+    tcopy = [remote(tb.at[t], tin.at[t // 2], ts.at[t // 2], tr.at[t // 2], sib) for t in (1, 3)]
     bcopy = [remote(pbuf.at[t], inbuf.at[t], bs.at[t], br.at[t], up_id) for t in range(SLABS - 1)]
 
     def to_parts(t):
@@ -224,39 +234,52 @@
     ex[2].wait()
     bcopy[SLABS - 2].wait_recv()
 
-    rot_x = rot[:2 * half]
-    rot_r = rot[2 * half:4 * half]
-    rot_p = rot[4 * half:]
+    loc_rot.wait()
+    n = 2 * half
+    ct_hi, ct_lo = split(jnp.concatenate(
+        [rotv[...], jnp.where(lax.broadcasted_iota(jnp.int32, (n, 3 * n), 1) < n, 0.0, rotv[...])], axis=0))
+    ct = jnp.concatenate([ct_hi, ct_lo], axis=0)
     for j in range(L // CH):
         at = slice(j * CH, (j + 1) * CH)
         x = xw[0, :, at]
         res = hx[:, at] + inbuf[SLABS - 2, :, at] - jnp.concatenate([lam[...]] * (CH // W), axis=1) * x
-        zp = mm_high(rot_r, res, TN) + mm_high(rot_p, pv[:, at], TN)
-        z = zp + mm_high(rot_x, x, TN)
-        ostage[1, :, at] = zp
-        zw[0, :, at] = z
-        hi, lo = split(z)
-        zz[:2 * half, at] = hi
-        zz[2 * half:, at] = lo
-    zcopy[0].start()
+        r_hi, r_lo = split(res)
+        p_hi, p_lo = split(pv[:, at])
+        b_hi = jnp.concatenate([xx[0, :n, at], r_hi, p_hi], axis=0)
+        b_lo = jnp.concatenate([xx[0, n:, at], r_lo, p_lo], axis=0)
+        both = mm(ct, b_hi, NN)
+        both = both[:2 * n] + both[2 * n:] + mm(ct_hi, b_lo, NN)
+        zw[0, :, at] = both[:n]
+        hi, lo = split(both[:n])
+        zz[:n, at] = hi
+        zz[n:, at] = lo
+        hi, lo = split(both[n:])
+        zzp[:n, at] = hi
+        zzp[n:, at] = lo
+    for c in zcopy:
+        c.start()
+
+    def sum_copies(which, g):
+        m, c, member, (buf, ssem, rsem) = groups[g]
+        return [
+            remote(buf.at[which, c], buf.at[which, c], ssem.at[which, k - 1], rsem.at[which, k - 1],
+                   member(lax.rem(c + k, m)))
+            for k in range(1, m)
+        ]
 
     def sum_start(which, g, value):
-        m, c, member = groups[g]
-        buf = arbuf.at[which, g]
-        buf[c] = value
+        m, c, member, (buf, ssem, rsem) = groups[g]
+        buf[which, c] = value
+        for copy in sum_copies(which, g):
+            copy.start()
+
+    def sum_finish(which, g):
+        m, c, member, (buf, ssem, rsem) = groups[g]
+        for copy in sum_copies(which, g):
+            copy.wait()
+        total = buf[which, 0]
         for k in range(1, m):
-            remote(buf.at[c], buf.at[c], ars.at[which, g, k - 1], arr.at[which, g, k - 1],
-                   member(lax.rem(c + k, m))).start()
-
-    def sum_finish(which, g):
-        m, c, member = groups[g]
-        buf = arbuf.at[which, g]
-        for k in range(1, m):
-            remote(buf.at[c], buf.at[c], ars.at[which, g, k - 1], arr.at[which, g, k - 1],
-                   member(lax.rem(c + k, m))).wait()
-        total = buf[0]
-        for k in range(1, m):
-            total = total + buf[k]
+            total = total + buf[which, k]
         return total
 
     def z_times_m(t):
@@ -264,38 +287,52 @@
             tb[t, :, at] = v
         times_m(zz, t, put)
 
-    def z_next(t):
-        zcopy[t].wait_recv()
-        if t + 1 < SLABS - 1:
-            zcopy[t + 1].start()
-
-    def s_part(t):
-        return mm_high(tb[t], zw[t], NT)
+    def quarters(v):
+        return v[:n, :n] + v[:n, n:] + v[n:, :n] + v[n:, n:]
+
+    def s_part(k):
+        if k:
+            zcopy[k - 1].wait_recv()
+            hi, lo = split(zw[k])
+            other_z = jnp.concatenate([hi, lo], axis=0)
+        else:
+            other_z = zz[...]
+        hi, lo = split(tb[2 * k])
+        return mm(jnp.concatenate([hi, lo], axis=0), other_z, NT)
 
     def fold(v):
         return jnp.concatenate([v[:half], v[half:]], axis=1)
 
     def unfold(v):
-        return jnp.concatenate([v[:, :2 * half], v[:, 2 * half:]], axis=0)
-
-    sum_start(0, 0, fold(mm_high(zw[0], zw[0], NT)))
+        return jnp.concatenate([v[:, :n], v[:, n:]], axis=0)
+
+    sum_start(0, 0, fold(quarters(mm(zz[...], zz[...], NT))))
+    z_times_m(1)
+    tcopy[0].start()
+    z_times_m(3)
+    tcopy[1].start()
     z_times_m(0)
     sum_start(0, 1, sum_finish(0, 0))
-    z_next(0)
-    z_times_m(1)
-    sum_start(0, 2, sum_finish(0, 1))
-    z_next(1)
     z_times_m(2)
-    sum_start(0, 3, sum_finish(0, 2))
-    z_times_m(3)
-    z_next(2)
-    small = unfold(sum_finish(0, 3)) * (1.0 / ntot)
+    z_times_m(4)
+    tcopy[0].wait_recv()
+    tb[2 * (1 - h)] += tin[0]
+    tcopy[1].wait_recv()
+    tb[2 * (2 - h)] += tin[1]
+    s = s_part(0)
+    s = s + s_part(1)
+    s = s + s_part(2)
+    sum_start(1, 0, fold(quarters(s)))
+    small = unfold(sum_finish(0, 1)) * (1.0 / ntot)
     li = inverse_factor(small)
-    z_times_m(4)
+    sum_start(1, 1, sum_finish(1, 0))
+    li_hi, li_lo = split(li)
+    ll = jnp.concatenate([jnp.concatenate([li_hi, li_hi], axis=1), jnp.concatenate([li_lo, li_lo], axis=1)], axis=0)
     for j in range(L // CH):
         at = slice(j * CH, (j + 1) * CH)
-        ostage[0, :, at] = mm_high(li, zw[0, :, at], NN)
-        ostage[1, :, at] = mm_high(li, ostage[1, :, at], NN)
+        for k, src in enumerate((zz, zzp)):
+            v = mm(ll, src[:, at], NN)
+            ostage[k, :, at] = v[:n] + v[n:]
     orows = pl.multiple_of((1 - h) * half, half)
     ocopy = []
     for k, out in enumerate((nc, nd)):
@@ -303,21 +340,18 @@
         ocopy.append(pltpu.make_async_copy(ostage.at[k, pl.ds(hrows, half)], out.at[:, pl.ds(mine, L)], loc_sem.at[2 + k]))
     for c in ocopy:
         c.start()
-    s = s_part(0)
-    for t in range(1, SLABS - 1):
-        s = s + s_part(t)
-    z_next(SLABS - 2)
-    s = s + s_part(SLABS - 1)
-    sum_start(1, 0, fold(s))
-    for g in range(1, len(groups)):
-        sum_start(1, g, sum_finish(1, g - 1))
-    s = unfold(sum_finish(1, len(groups) - 1)) * (1.0 / ntot)
+    s = unfold(sum_finish(1, 1)) * (1.0 / ntot)
     sym = s + jnp.transpose(s)
     proj[...] = mm_high(mm_high(li, sym, NN), li, NT)
     for c in ocopy:
         c.wait()
-    for c in xcopy + zcopy + bcopy:
+    for c in xcopy + zcopy + bcopy + tcopy:
         c.wait_send()
+
+
+def place(*refs):
+    for k in range(3):
+        refs[3 + k][...] = refs[k][...]
 
 
 def on_device(dims, ntot, blocks, columns, current, directions, ritz_values, rotation):
@@ -333,8 +367,8 @@
     any_ = pl.BlockSpec(memory_space=pl.ANY)
     vmem = pl.BlockSpec(memory_space=pltpu.VMEM)
     smem = pl.BlockSpec(memory_space=pltpu.SMEM)
-    n_groups = 1 + len(dims)
-    most = max((2,) + tuple(dims))
+    ga = 2 * dims[-1]
+    gb = total_rows // rows_here // dims[-1]
     dma = pltpu.SemaphoreType.DMA
     hops = SLABS - 1
     scratch = [pltpu.VMEM((slots + 1, W, W), F32) for _ in range(RB)] + [
@@ -342,35 +376,47 @@
         pltpu.VMEM((L, SLABS * L), BF16),
         pltpu.VMEM((SLABS, states, L), F32),
         pltpu.VMEM((SLABS, 2 * states, L), BF16),
-        pltpu.VMEM((SLABS, states, L), F32),
+        pltpu.VMEM((3, states, L), F32),
+        pltpu.VMEM((2 * states, L), BF16),
         pltpu.VMEM((2 * states, L), BF16),
         pltpu.VMEM((hops, states, L), F32),
         pltpu.VMEM((hops, states, L), F32),
         pltpu.VMEM((SLABS, states, L), F32),
+        pltpu.VMEM((2, states, L), F32),
         pltpu.VMEM((states, L), F32),
         pltpu.VMEM((states, L), F32),
         pltpu.VMEM((states, W), F32),
+        pltpu.VMEM((states, 3 * states), F32),
+        pltpu.VMEM((1, half), F32),
         pltpu.VMEM((2, states, L), F32),
-        pltpu.VMEM((2, n_groups, most, half, 2 * states), F32),
-        dma((RB,)), dma((4,)), dma((3,)), dma((3,)),
-        dma((hops,)), dma((hops,)), dma((hops,)), dma((hops,)), dma((hops,)), dma((hops,)),
-        dma((2, n_groups, most)), dma((2, n_groups, most)), dma((2,)), dma((2,)),
+        pltpu.VMEM((2, ga, half, 2 * states), F32),
+        pltpu.VMEM((2, gb, half, 2 * states), F32),
+        dma((RB,)), dma((6,)), dma((3,)), dma((3,)),
+        dma((hops,)), dma((hops,)), dma((2,)), dma((2,)), dma((2,)), dma((2,)), dma((hops,)), dma((hops,)),
+        dma((2, ga)), dma((2, ga)), dma((2, gb)), dma((2, gb)), dma((2,)), dma((2,)),
     ]
-    return pl.pallas_call(
+    outs = pl.pallas_call(
         functools.partial(kernel, dims, ntot),
         out_shape=(
             jax.ShapeDtypeStruct((half, length), F32),
             jax.ShapeDtypeStruct((half, length), F32),
             jax.ShapeDtypeStruct((states, states), F32),
         ),
-        in_specs=[smem, any_, any_, any_, vmem, vmem],
+        in_specs=[smem, any_, any_, any_, any_, any_],
         out_specs=(any_, any_, vmem),
         scratch_shapes=scratch,
         compiler_params=pltpu.CompilerParams(
             collective_id=0, has_side_effects=True, vmem_limit_bytes=58 * 2**20
         ),
         name="lobpcg",
-    )(inv, blocks, current, directions, ritz_values.reshape(1, half), rotation)
+    )(inv, blocks, current, directions, ritz_values.reshape(1, half), rotation.T)
+    return pl.pallas_call(
+        place,
+        out_shape=tuple(jax.ShapeDtypeStruct(o.shape, o.dtype) for o in outs),
+        in_specs=[vmem] * 3,
+        out_specs=(vmem,) * 3,
+        name="place",
+    )(*outs)
 
 
 def solution(mesh):

time: 91.1 us -> 77.3 us (0.85)
  the two profiles are of different devices: /device:TPU:1 before, /device:TPU:0 now
where the time goes in v2:
time: 77.3 us; the launch traced here: 77.1 us
  Pallas kernels  74.8 us (97%)
  other arithmetic  1.54 us (2%)
    pallas_call x1, Pallas kernels, on_device(): pl.pallas_call(functools.partial(kernel, dims, ntot), out_shape=(jax.Shap...  72.9 us
    pallas_call x1, Pallas kernels, on_device(): pl.pallas_call(place, out_shape=tuple((jax.ShapeDtypeStruct(o.shape, o.dt...  1.84 us

profile of v2, /device:TPU:0, one launch (start us, length us, event | category | flops | bytes accessed | tf_op | source)
XLA Modules:
  0.0 77.1 jit_solution(14587901701264976458)
XLA Ops:
  0.7 0.8 %add_select_fusion = s32[16,25]{1,0:T(8,128)S(1)} fusion(s32[16,25]{1,0:T(8,128)} %param.7, s32[16]{0:T(128)S(1)} %iota_add_fusion.1), kind=kLoop, calls=%fused_computation.2 | loop fusion | flops 4800 | bytes 3264 | tf_op jit(solution)/shard_map/jit(remainder)/select_n | solution.py:363
  1.4 0.1 copy.9
  1.5 0.1 select_reduce_fusion
  1.7 0.6 broadcast_add_fusion.inv_ref
  2.3 72.9 %lobpcg.1 = (f32[32,2048]{1,0:T(8,128)}, f32[32,2048]{1,0:T(8,128)}, f32[64,64]{1,0:T(8,128)}) custom-call(s32[16,33]{1,0:T(8,128)} %broadcast_add_fusion.inv_ref, f32[16,25,128,128]{3,2,1,0:T(8,128)} %blocks.1, f32[32,2048]{1,0:T(8,128)} %current.1, f32[32,2048]{1,0:T(8,128)} %directions.1, f32[1,32]{1,0:T(1,128)} %bitcast.3, f32[64,192]{1,0:T(8,128)} %bitcast.2), custom_call_target="tpu_custom_call" | custom-call | tf_op jit(solution)/shard_map/lobpcg/pallas_call | solution.py:398
  75.2 1.8 %place.1 = (f32[32,2048]{1,0:T(8,128)}, f32[32,2048]{1,0:T(8,128)}, f32[64,64]{1,0:T(8,128)}) custom-call(f32[32,2048]{1,0:T(8,128)} %get-tuple-element.6.refs_0_, f32[32,2048]{1,0:T(8,128)} %get-tuple-element.7.refs_1_, f32[64,64]{1,0:T(8,128)} %get-tuple-element.8.refs_2_), custom_call_target="tpu_custom_call" | custom-call | tf_op jit(solution)/shard_map/place/pallas_call | solution.py:413
  (2 shorter events, 0.0 us)

commit v3 on v2

--- a/solution.py
+++ b/solution.py
@@ -36,42 +36,49 @@
     return hi, (v - hi.astype(F32)).astype(BF16)
 
 
-def inverse_factor(g):
+def factor_start(g):
     n = g.shape[0]
     rows = lax.broadcasted_iota(jnp.int32, (n, 2 * n), 0)
     lanes = lax.broadcasted_iota(jnp.int32, (n, 2 * n), 1)
-    eye = jnp.where(rows + n == lanes, 1.0, 0.0).astype(F32)
-    a = jnp.concatenate([g, jnp.zeros((n, n), F32)], axis=1) + eye
-
-    def step(k, a):
-        row = jnp.sum(jnp.where(rows == k, a, 0.0), axis=0, keepdims=True)
-        col = jnp.sum(jnp.where(lanes == k, a, 0.0), axis=1, keepdims=True)
-        pivot = jnp.sum(jnp.where(lanes[:1] == k, row, 0.0), axis=1, keepdims=True)
-        factor = jnp.where(rows[:, :1] > k, col / pivot, 0.0)
-        return a - factor * row
-
-    a = lax.fori_loop(0, n, step, a)
+    a = jnp.concatenate([g, jnp.zeros((n, n), F32)], axis=1) + jnp.where(rows + n == lanes, 1.0, 0.0).astype(F32)
+    return [a[8 * i:8 * i + 8] for i in range(n // 8)]
+
+
+def factor_steps(a, first, last):
+    a = list(a)
+    sub = lax.broadcasted_iota(jnp.int32, (8, 1), 0)
+    for k in range(first, last):
+        b, s = divmod(k, 8)
+        row = a[b][s:s + 1, :]
+        scaled = row * (1.0 / row[:, k:k + 1])
+        for i in range(b, len(a)):
+            col = a[i][:, k:k + 1]
+            if i == b:
+                col = jnp.where(sub > s, col, 0.0)
+            a[i] = a[i] - col * scaled
+    return a
+
+
+def factor_end(a):
+    a = jnp.concatenate(a, axis=0)
+    n = a.shape[0]
+    rows = lax.broadcasted_iota(jnp.int32, (n, 2 * n), 0)
+    lanes = lax.broadcasted_iota(jnp.int32, (n, 2 * n), 1)
     diag = jnp.sum(jnp.where(rows == lanes, a, 0.0), axis=1, keepdims=True)
     return a[:, n:] * (1.0 / jnp.sqrt(diag))
 
 
 def kernel(dims, ntot, inv_ref, blocks, current, directions, ritz, rot, nc, nd, proj, *scratch):
     stages = scratch[:RB]
-    (mh, ml, xw, xx, zw, zz, zzp, pbuf, inbuf, tb, tin, hx, pv, lam, rotv, ritzv, ostage, bufa, bufb,
-     blk_sem, loc_sem, exs, exr, xs, xr, zs, zr, ts, tr, bs, br, asa, ara, asb, arb, outs, outr) = scratch[RB:]
+    (mh, ml, xw, xx, zw, zz, zzp, part, inbuf, tb, tin, hx, pv, lam, rotv, ritzv, ostage, bufa, bufb,
+     blk_sem, loc_sem, exs, exr, xs, xr, cs, cr, zs, zr, ts, tr, bs, br, asa, ara, asb, arb, outs, outr) = scratch[RB:]
     half, full = current.shape
     slots = blocks.shape[1]
     rows_n = 1
     for m in dims:
         rows_n *= m
-    units = 2 * rows_n
     r = lax.axis_index("row")
     h = lax.axis_index("col")
-    u = 2 * r + h
-    down = lax.rem(u + units - 1, units)
-    up = lax.rem(u + 1, units)
-    down_id = (down // 2, lax.rem(down, 2))
-    up_id = (up // 2, lax.rem(up, 2))
     sib = (r, 1 - h)
 
     ny = dims[-1]
@@ -92,7 +99,7 @@
     mine = pl.multiple_of(h * L, L)
     other = pl.multiple_of((1 - h) * L, L)
     hrows = pl.multiple_of(h * half, half)
-    loc_x = pltpu.make_async_copy(current.at[:, pl.ds(mine, L)], xw.at[0, pl.ds(hrows, half)], loc_sem.at[0])
+    loc_x = pltpu.make_async_copy(current.at[:, pl.ds(mine, L)], xw.at[h, pl.ds(hrows, half)], loc_sem.at[0])
     loc_x.start()
     loc_p = pltpu.make_async_copy(directions.at[:, pl.ds(mine, L)], pv.at[pl.ds(hrows, half)], loc_sem.at[1])
     loc_p.start()
@@ -102,7 +109,7 @@
     loc_ritz.start()
 
     barrier = pltpu.get_barrier_semaphore()
-    partners = [down_id, up_id] + [row_at(k) for k in (-2, -1, 1, 2)]
+    partners = [row_at(k) for k in (-2, -1, 1, 2)]
     for m, c, member, _ in groups:
         for k in range(1, m):
             partners.append(member(lax.rem(c + k, m)))
@@ -127,19 +134,22 @@
             src_ref=src, dst_ref=dst, send_sem=ssem, recv_sem=rsem, device_id=dev, device_id_type=MESH)
 
     ex = [
-        remote(current.at[:, pl.ds(other, L)], xw.at[0, pl.ds(hrows, half)], exs.at[0], exr.at[0], sib),
+        remote(current.at[:, pl.ds(other, L)], xw.at[1 - h, pl.ds(hrows, half)], exs.at[0], exr.at[0], sib),
         remote(directions.at[:, pl.ds(other, L)], pv.at[pl.ds(hrows, half)], exs.at[1], exr.at[1], sib),
         remote(lam.at[pl.ds(hrows, half)], lam.at[pl.ds(hrows, half)], exs.at[2], exr.at[2], sib),
     ]
     for c in ex:
         c.start()
-    xcopy = [remote(xw.at[t], xw.at[t + 1], xs.at[t], xr.at[t], down_id) for t in range(SLABS - 1)]
-    zcopy = [remote(zw.at[0], zw.at[k], zs.at[k - 1], zr.at[k - 1], row_at(-k)) for k in (1, 2)]
-    tcopy = [remote(tb.at[t], tin.at[t // 2], ts.at[t // 2], tr.at[t // 2], sib) for t in (1, 3)]
-    bcopy = [remote(pbuf.at[t], inbuf.at[t], bs.at[t], br.at[t], up_id) for t in range(SLABS - 1)]
+    xcopy = [remote(xw.at[h], xw.at[h + 2 * k], xs.at[k - 1], xr.at[k - 1], row_at(-k)) for k in (1, 2)]
+    shared = [remote(xw.at[w], xw.at[w], cs.at[k], cr.at[k], sib) for k, w in enumerate((1, 2 + h, 4))]
+    got = remote(xw.at[3 - h], xw.at[3 - h], cs.at[1], cr.at[1], sib)
+    zcopy = remote(zw.at[0], zw.at[1], zs, zr, row_at(-1))
+    tcopy = [remote(tb.at[t], tin.at[k], ts.at[k], tr.at[k], dev) for k, (t, dev) in enumerate(((1, sib), (3, sib), (4, row_at(1))))]
+    scopy = [remote(part.at[t], inbuf.at[t], bs.at[t], br.at[t], sib) for t in (1, 3)]
+    bcopy = [remote(part.at[t], inbuf.at[t], bs.at[t], br.at[t], row_at(t // 2)) for t in (2, 4)]
 
     def to_parts(t):
-        hi, lo = split(xw[t])
+        hi, lo = split(xw[h + t])
         xx[t, :2 * half] = hi
         xx[t, 2 * half:] = lo
 
@@ -193,46 +203,65 @@
             lax.fori_loop(0, L // CH, body, 0)
 
     def back(t):
-        s = SLABS - 1 - t
         def put(at, v):
-            pbuf[s, :, at] = v
+            part[t, :, at] = v
         times_m(xx.at[0], t, put)
-        if s > 0:
-            bcopy[s - 1].wait_recv()
-            pbuf[s] += inbuf[s - 1]
-        bcopy[s].start()
 
     loc_x.wait()
+    for i in range(RB // 2):
+        expand(i)
     ex[0].wait()
-    xcopy[0].start()
+    for c in xcopy:
+        c.start()
+    pl.when(h == 1)(shared[0].start)
+    for i in range(RB // 2, RB):
+        expand(i)
     to_parts(0)
-    for i in range(RB):
-        expand(i)
-        if i == RB // 2:
-            xcopy[0].wait_recv()
-            xcopy[1].start()
+    back(3)
+    scopy[1].start()
     back(4)
-    xcopy[1].wait_recv()
-    xcopy[2].start()
-    back(3)
-    xcopy[2].wait_recv()
-    xcopy[3].start()
+    scopy[1].wait_recv()
+
+    @pl.when(h == 0)
+    def _():
+        part[4] += inbuf[3]
+    bcopy[1].start()
+    back(1)
+    scopy[0].start()
     back(2)
-    back(1)
+    scopy[0].wait_recv()
+    part[2] += inbuf[3 - 2 * (1 - h)]
+    bcopy[0].start()
 
     def put_hx(at, v):
         hx[:, at] = v
     times_m(xx.at[0], 0, put_hx)
+    xcopy[0].wait_recv()
+    shared[1].start()
     times_mt(0)
-    for t in range(1, SLABS):
-        if t == SLABS - 1:
-            xcopy[t - 1].wait_recv()
-        to_parts(t)
-        times_mt(t)
+    pl.when(h == 0)(shared[0].wait_recv)
+    pl.when(h == 1)(got.wait_recv)
+    to_parts(1)
+    times_mt(1)
+    to_parts(2)
+    times_mt(2)
+    xcopy[1].wait_recv()
+    pl.when(h == 0)(shared[2].start)
+    to_parts(4)
+    times_mt(4)
+    pl.when(h == 0)(got.wait_recv)
+    pl.when(h == 1)(shared[2].wait_recv)
+    to_parts(3)
+    times_mt(3)
     loc_p.wait()
     ex[1].wait()
     ex[2].wait()
-    bcopy[SLABS - 2].wait_recv()
+    for c in bcopy:
+        c.wait_recv()
+
+    @pl.when(h == 1)
+    def _():
+        hx[...] += inbuf[1]
 
     loc_rot.wait()
     n = 2 * half
@@ -241,8 +270,8 @@
     ct = jnp.concatenate([ct_hi, ct_lo], axis=0)
     for j in range(L // CH):
         at = slice(j * CH, (j + 1) * CH)
-        x = xw[0, :, at]
-        res = hx[:, at] + inbuf[SLABS - 2, :, at] - jnp.concatenate([lam[...]] * (CH // W), axis=1) * x
+        x = xw[h, :, at]
+        res = hx[:, at] + inbuf[2, :, at] + inbuf[4, :, at] - jnp.concatenate([lam[...]] * (CH // W), axis=1) * x
         r_hi, r_lo = split(res)
         p_hi, p_lo = split(pv[:, at])
         b_hi = jnp.concatenate([xx[0, :n, at], r_hi, p_hi], axis=0)
@@ -256,8 +285,6 @@
         hi, lo = split(both[n:])
         zzp[:n, at] = hi
         zzp[n:, at] = lo
-    for c in zcopy:
-        c.start()
 
     def sum_copies(which, g):
         m, c, member, (buf, ssem, rsem) = groups[g]
@@ -292,7 +319,6 @@
 
     def s_part(k):
         if k:
-            zcopy[k - 1].wait_recv()
             hi, lo = split(zw[k])
             other_z = jnp.concatenate([hi, lo], axis=0)
         else:
@@ -307,25 +333,38 @@
         return jnp.concatenate([v[:, :n], v[:, n:]], axis=0)
 
     sum_start(0, 0, fold(quarters(mm(zz[...], zz[...], NT))))
+    zcopy.start()
+    z_times_m(3)
+    tcopy[1].start()
+    z_times_m(4)
+    tcopy[1].wait_recv()
+
+    @pl.when(h == 0)
+    def _():
+        tb[4] += tin[1]
+    tcopy[2].start()
     z_times_m(1)
     tcopy[0].start()
-    z_times_m(3)
-    tcopy[1].start()
+    sum_start(0, 1, sum_finish(0, 0))
     z_times_m(0)
-    sum_start(0, 1, sum_finish(0, 0))
     z_times_m(2)
-    z_times_m(4)
     tcopy[0].wait_recv()
     tb[2 * (1 - h)] += tin[0]
-    tcopy[1].wait_recv()
-    tb[2 * (2 - h)] += tin[1]
+
+    @pl.when(h == 1)
+    def _():
+        tb[2] += tin[1]
     s = s_part(0)
+    zcopy.wait_recv()
+    tcopy[2].wait_recv()
+    tb[2] += tin[2]
     s = s + s_part(1)
-    s = s + s_part(2)
     sum_start(1, 0, fold(quarters(s)))
-    small = unfold(sum_finish(0, 1)) * (1.0 / ntot)
-    li = inverse_factor(small)
+    a = factor_start(unfold(sum_finish(0, 1)) * (1.0 / ntot))
+    a = factor_steps(a, 0, half)
     sum_start(1, 1, sum_finish(1, 0))
+    a = factor_steps(a, half, n)
+    li = factor_end(a)
     li_hi, li_lo = split(li)
     ll = jnp.concatenate([jnp.concatenate([li_hi, li_hi], axis=1), jnp.concatenate([li_lo, li_lo], axis=1)], axis=0)
     for j in range(L // CH):
@@ -345,8 +384,10 @@
     proj[...] = mm_high(mm_high(li, sym, NN), li, NT)
     for c in ocopy:
         c.wait()
-    for c in xcopy + zcopy + bcopy + tcopy:
+    for c in xcopy + shared[1:2] + [zcopy] + scopy + bcopy + tcopy:
         c.wait_send()
+    pl.when(h == 1)(shared[0].wait_send)
+    pl.when(h == 0)(shared[2].wait_send)
 
 
 def place(*refs):
@@ -370,19 +411,18 @@
     ga = 2 * dims[-1]
     gb = total_rows // rows_here // dims[-1]
     dma = pltpu.SemaphoreType.DMA
-    hops = SLABS - 1
     scratch = [pltpu.VMEM((slots + 1, W, W), F32) for _ in range(RB)] + [
         pltpu.VMEM((L, SLABS * L), BF16),
         pltpu.VMEM((L, SLABS * L), BF16),
-        pltpu.VMEM((SLABS, states, L), F32),
+        pltpu.VMEM((SLABS + 1, states, L), F32),
         pltpu.VMEM((SLABS, 2 * states, L), BF16),
-        pltpu.VMEM((3, states, L), F32),
+        pltpu.VMEM((2, states, L), F32),
         pltpu.VMEM((2 * states, L), BF16),
         pltpu.VMEM((2 * states, L), BF16),
-        pltpu.VMEM((hops, states, L), F32),
-        pltpu.VMEM((hops, states, L), F32),
         pltpu.VMEM((SLABS, states, L), F32),
-        pltpu.VMEM((2, states, L), F32),
+        pltpu.VMEM((SLABS, states, L), F32),
+        pltpu.VMEM((SLABS, states, L), F32),
+        pltpu.VMEM((3, states, L), F32),
         pltpu.VMEM((states, L), F32),
         pltpu.VMEM((states, L), F32),
         pltpu.VMEM((states, W), F32),
@@ -392,7 +432,8 @@
         pltpu.VMEM((2, ga, half, 2 * states), F32),
         pltpu.VMEM((2, gb, half, 2 * states), F32),
         dma((RB,)), dma((6,)), dma((3,)), dma((3,)),
-        dma((hops,)), dma((hops,)), dma((2,)), dma((2,)), dma((2,)), dma((2,)), dma((hops,)), dma((hops,)),
+        dma((2,)), dma((2,)), dma((3,)), dma((3,)), dma(()), dma(()), dma((3,)), dma((3,)),
+        dma((SLABS,)), dma((SLABS,)),
         dma((2, ga)), dma((2, ga)), dma((2, gb)), dma((2, gb)), dma((2,)), dma((2,)),
     ]
     outs = pl.pallas_call(

time: 77.3 us -> 67.6 us (0.87)
  the two profiles are of different devices: /device:TPU:0 before, /device:TPU:1 now
where the time goes in v3:
time: 67.6 us; the launch traced here: 66.7 us
  Pallas kernels  64.4 us (95%)
  other arithmetic  1.54 us (2%)
    pallas_call x1, Pallas kernels, on_device(): pl.pallas_call(functools.partial(kernel, dims, ntot), out_shape=(jax.Shap...  62.5 us
    pallas_call x1, Pallas kernels, on_device(): pl.pallas_call(place, out_shape=tuple((jax.ShapeDtypeStruct(o.shape, o.dt...  1.84 us

profile of v3, /device:TPU:1, one launch (start us, length us, event | category | flops | bytes accessed | tf_op | source)
XLA Modules:
  0.0 66.7 jit_solution(6560616603062299733)
XLA Ops:
  0.7 0.8 %add_select_fusion = s32[16,25]{1,0:T(8,128)S(1)} fusion(s32[16,25]{1,0:T(8,128)} %param.7, s32[16]{0:T(128)S(1)} %iota_add_fusion.1), kind=kLoop, calls=%fused_computation.2 | loop fusion | flops 4800 | bytes 3264 | tf_op jit(solution)/shard_map/jit(remainder)/select_n | solution.py:404
  1.4 0.1 copy.9
  1.5 0.1 select_reduce_fusion
  1.7 0.6 broadcast_add_fusion.inv_ref
  2.3 62.5 %lobpcg.1 = (f32[32,2048]{1,0:T(8,128)}, f32[32,2048]{1,0:T(8,128)}, f32[64,64]{1,0:T(8,128)}) custom-call(s32[16,33]{1,0:T(8,128)} %broadcast_add_fusion.inv_ref, f32[16,25,128,128]{3,2,1,0:T(8,128)} %blocks.1, f32[32,2048]{1,0:T(8,128)} %current.1, f32[32,2048]{1,0:T(8,128)} %directions.1, f32[1,32]{1,0:T(1,128)} %bitcast.3, f32[64,192]{1,0:T(8,128)} %bitcast.2), custom_call_target="tpu_custom_call" | custom-call | tf_op jit(solution)/shard_map/lobpcg/pallas_call | solution.py:439
  64.8 1.8 %place.1 = (f32[32,2048]{1,0:T(8,128)}, f32[32,2048]{1,0:T(8,128)}, f32[64,64]{1,0:T(8,128)}) custom-call(f32[32,2048]{1,0:T(8,128)} %get-tuple-element.6.refs_0_, f32[32,2048]{1,0:T(8,128)} %get-tuple-element.7.refs_1_, f32[64,64]{1,0:T(8,128)} %get-tuple-element.8.refs_2_), custom_call_target="tpu_custom_call" | custom-call | tf_op jit(solution)/shard_map/place/pallas_call | solution.py:454
  (2 shorter events, 0.0 us)

commit v4 on v3

--- a/solution.py
+++ b/solution.py
@@ -68,10 +68,10 @@
     return a[:, n:] * (1.0 / jnp.sqrt(diag))
 
 
-def kernel(dims, ntot, inv_ref, blocks, current, directions, ritz, rot, nc, nd, proj, *scratch):
+def kernel(dims, ntot, columns, blocks, current, directions, ritz, rot, nc, nd, proj, *scratch):
     stages = scratch[:RB]
-    (mh, ml, xw, xx, zw, zz, zzp, part, inbuf, tb, tin, hx, pv, lam, rotv, ritzv, ostage, bufa, bufb,
-     blk_sem, loc_sem, exs, exr, xs, xr, cs, cr, zs, zr, ts, tr, bs, br, asa, ara, asb, arb, outs, outr) = scratch[RB:]
+    (mh, ml, xw, xx, zw, zz, zzp, part, inbuf, tb, tin, hx, pv, lam, rotv, ritzv, colv, invv, inv_ref, xo, ostage, bufa, bufb,
+     blk_sem, loc_sem, exs, exr, xs, xr, cs, cr, zs, zr, ts, tr, ss, sr, bs, br, asa, ara, asb, arb, outs, outr) = scratch[RB:]
     half, full = current.shape
     slots = blocks.shape[1]
     rows_n = 1
@@ -91,6 +91,14 @@
 
     def row_at(k):
         return (lax.rem(r + k + rows_n, rows_n), h)
+
+    barrier = pltpu.get_barrier_semaphore()
+    partners = [row_at(k) for k in (-1, 1)]
+    for m, c, member, _ in groups:
+        for k in range(1, m):
+            partners.append(member(lax.rem(c + k, m)))
+    for d in partners:
+        pl.semaphore_signal(barrier, inc=1, device_id=d, device_id_type=MESH)
 
     for i in range(RB):
         pltpu.make_async_copy(
@@ -103,23 +111,15 @@
     loc_x.start()
     loc_p = pltpu.make_async_copy(directions.at[:, pl.ds(mine, L)], pv.at[pl.ds(hrows, half)], loc_sem.at[1])
     loc_p.start()
+    loc_xo = pltpu.make_async_copy(current.at[:, pl.ds(other, L)], xo, loc_sem.at[8])
+    loc_xo.start()
     loc_rot = pltpu.make_async_copy(rot, rotv, loc_sem.at[4])
     loc_rot.start()
     loc_ritz = pltpu.make_async_copy(ritz, ritzv, loc_sem.at[5])
     loc_ritz.start()
-
-    barrier = pltpu.get_barrier_semaphore()
-    partners = [row_at(k) for k in (-2, -1, 1, 2)]
-    for m, c, member, _ in groups:
-        for k in range(1, m):
-            partners.append(member(lax.rem(c + k, m)))
-    for d in partners:
-        pl.semaphore_signal(barrier, inc=1, device_id=d, device_id_type=MESH)
-
-    er = lax.broadcasted_iota(jnp.int32, (half, half), 0) == lax.broadcasted_iota(jnp.int32, (half, half), 1)
-    loc_ritz.wait()
-    lam_own = jnp.sum(jnp.where(er, jnp.broadcast_to(ritzv[...], (half, half)), 0.0), axis=1, keepdims=True)
-    lam[pl.ds(hrows, half), :] = jnp.broadcast_to(lam_own, (half, W))
+    loc_col = pltpu.make_async_copy(columns, colv, loc_sem.at[6])
+    loc_col.start()
+
     for i in range(RB):
         stages[i][slots] = jnp.zeros((W, W), F32)
     zero = jnp.zeros((W, W), BF16)
@@ -127,6 +127,19 @@
         for m_ref in (mh, ml):
             m_ref[(j + 1) * W:(j + 2) * W, j * W:(j + 1) * W] = zero
             m_ref[j * W:(j + 1) * W, (WB + j + 1) * W:(WB + j + 2) * W] = zero
+    loc_col.wait()
+    at = lax.broadcasted_iota(jnp.int32, (RB, slots), 0) + (2 * r + h) * RB
+    ahead = colv[pl.ds(pl.multiple_of(h * RB, RB), RB), :] - at
+    ahead = jnp.where(ahead < 0, ahead + rows_n * 2 * RB, ahead)
+    lanes = lax.broadcasted_iota(jnp.int32, (RB, W), 1)
+    found = jnp.full((RB, W), slots, jnp.int32)
+    for k in range(slots):
+        found = jnp.where(ahead[:, k:k + 1] == lanes, k, found)
+    invv[...] = found
+    to_smem = pltpu.make_async_copy(invv, inv_ref, loc_sem.at[7])
+    to_smem.start()
+    to_smem.wait()
+    loc_xo.wait()
     pl.semaphore_wait(barrier, len(partners))
 
     def remote(src, dst, ssem, rsem, dev):
@@ -134,19 +147,26 @@
             src_ref=src, dst_ref=dst, send_sem=ssem, recv_sem=rsem, device_id=dev, device_id_type=MESH)
 
     ex = [
-        remote(current.at[:, pl.ds(other, L)], xw.at[1 - h, pl.ds(hrows, half)], exs.at[0], exr.at[0], sib),
+        remote(xo, xw.at[1 - h, pl.ds(hrows, half)], exs.at[0], exr.at[0], sib),
         remote(directions.at[:, pl.ds(other, L)], pv.at[pl.ds(hrows, half)], exs.at[1], exr.at[1], sib),
         remote(lam.at[pl.ds(hrows, half)], lam.at[pl.ds(hrows, half)], exs.at[2], exr.at[2], sib),
     ]
-    for c in ex:
+    for c in ex[:2]:
         c.start()
-    xcopy = [remote(xw.at[h], xw.at[h + 2 * k], xs.at[k - 1], xr.at[k - 1], row_at(-k)) for k in (1, 2)]
+    piece = [pl.ds(c * half, half) for c in range(2)]
+
+    def pieces(src, i, dst, j, ssem, rsem, first, dev):
+        return [remote(src.at[i, p], dst.at[j, p], ssem.at[first + c], rsem.at[first + c], dev) for c, p in enumerate(piece)]
+
+    xown = pieces(xw, h, xw, h + 2, xs, xr, 0, row_at(-1))
+    xpass = pieces(xw, h + 2, xw, h + 4, xs, xr, 2, row_at(-1))
     shared = [remote(xw.at[w], xw.at[w], cs.at[k], cr.at[k], sib) for k, w in enumerate((1, 2 + h, 4))]
     got = remote(xw.at[3 - h], xw.at[3 - h], cs.at[1], cr.at[1], sib)
     zcopy = remote(zw.at[0], zw.at[1], zs, zr, row_at(-1))
     tcopy = [remote(tb.at[t], tin.at[k], ts.at[k], tr.at[k], dev) for k, (t, dev) in enumerate(((1, sib), (3, sib), (4, row_at(1))))]
-    scopy = [remote(part.at[t], inbuf.at[t], bs.at[t], br.at[t], sib) for t in (1, 3)]
-    bcopy = [remote(part.at[t], inbuf.at[t], bs.at[t], br.at[t], row_at(t // 2)) for t in (2, 4)]
+    scopy = [remote(part.at[t], inbuf.at[t], ss.at[t // 2], sr.at[t // 2], sib) for t in (1, 3)]
+    bown = pieces(part, 4, inbuf, 4, bs, br, 0, row_at(1))
+    bpass = pieces(part, 2, inbuf, 2, bs, br, 2, row_at(1))
 
     def to_parts(t):
         hi, lo = split(xw[h + t])
@@ -162,7 +182,7 @@
         ml[i * W:(i + 1) * W, i * W:(i + 1) * W] = lo
 
         def one(d, carry):
-            hi, lo = split(stages[i][inv_ref[h * RB + i, d]])
+            hi, lo = split(stages[i][inv_ref[i, d]])
             at = pl.multiple_of((i + d) * W, W)
             mh[i * W:(i + 1) * W, pl.ds(at, W)] = hi
             ml[i * W:(i + 1) * W, pl.ds(at, W)] = lo
@@ -184,7 +204,7 @@
             def body(j, carry):
                 chunk(j, 0, L)
                 return carry
-            lax.fori_loop(0, L // CH, body, 0)
+            lax.fori_loop(0, L // CH, body, 0, unroll=True)
 
     def times_mt(t):
         def chunk(j, lo, hi):
@@ -200,7 +220,7 @@
             def body(j, carry):
                 chunk(j, 0, L)
                 return carry
-            lax.fori_loop(0, L // CH, body, 0)
+            lax.fori_loop(0, L // CH, body, 0, unroll=True)
 
     def back(t):
         def put(at, v):
@@ -211,41 +231,65 @@
     for i in range(RB // 2):
         expand(i)
     ex[0].wait()
-    for c in xcopy:
+    for c in xown:
         c.start()
     pl.when(h == 1)(shared[0].start)
     for i in range(RB // 2, RB):
         expand(i)
     to_parts(0)
+    er = lax.broadcasted_iota(jnp.int32, (half, half), 0) == lax.broadcasted_iota(jnp.int32, (half, half), 1)
+    loc_ritz.wait()
+    lam_own = jnp.sum(jnp.where(er, jnp.broadcast_to(ritzv[...], (half, half)), 0.0), axis=1, keepdims=True)
+    lam[pl.ds(hrows, half), :] = jnp.broadcast_to(lam_own, (half, W))
+    ex[2].start()
     back(3)
     scopy[1].start()
     back(4)
-    scopy[1].wait_recv()
 
     @pl.when(h == 0)
     def _():
+        scopy[1].wait_recv()
         part[4] += inbuf[3]
-    bcopy[1].start()
+    for c in bown:
+        c.start()
     back(1)
     scopy[0].start()
     back(2)
-    scopy[0].wait_recv()
-    part[2] += inbuf[3 - 2 * (1 - h)]
-    bcopy[0].start()
+    xown[0].wait_recv()
+    xpass[0].start()
+
+    @pl.when(h == 0)
+    def _():
+        scopy[0].wait_recv()
+        part[2] += inbuf[1]
+
+    @pl.when(h == 1)
+    def _():
+        scopy[1].wait_recv()
+        part[2] += inbuf[3]
+
+    def pass_products(c):
+        bown[c].wait_recv()
+        part[2, piece[c]] += inbuf[4, piece[c]]
+        bpass[c].start()
 
     def put_hx(at, v):
         hx[:, at] = v
     times_m(xx.at[0], 0, put_hx)
-    xcopy[0].wait_recv()
+    times_mt(0)
+    xown[1].wait_recv()
+    xpass[1].start()
     shared[1].start()
-    times_mt(0)
     pl.when(h == 0)(shared[0].wait_recv)
     pl.when(h == 1)(got.wait_recv)
     to_parts(1)
     times_mt(1)
+    pass_products(0)
     to_parts(2)
     times_mt(2)
-    xcopy[1].wait_recv()
+    pass_products(1)
+    for c in xpass:
+        c.wait_recv()
     pl.when(h == 0)(shared[2].start)
     to_parts(4)
     times_mt(4)
@@ -256,12 +300,12 @@
     loc_p.wait()
     ex[1].wait()
     ex[2].wait()
-    for c in bcopy:
-        c.wait_recv()
-
     @pl.when(h == 1)
     def _():
+        scopy[0].wait_recv()
         hx[...] += inbuf[1]
+    for c in bpass:
+        c.wait_recv()
 
     loc_rot.wait()
     n = 2 * half
@@ -271,7 +315,7 @@
     for j in range(L // CH):
         at = slice(j * CH, (j + 1) * CH)
         x = xw[h, :, at]
-        res = hx[:, at] + inbuf[2, :, at] + inbuf[4, :, at] - jnp.concatenate([lam[...]] * (CH // W), axis=1) * x
+        res = hx[:, at] + inbuf[2, :, at] - jnp.concatenate([lam[...]] * (CH // W), axis=1) * x
         r_hi, r_lo = split(res)
         p_hi, p_lo = split(pv[:, at])
         b_hi = jnp.concatenate([xx[0, :n, at], r_hi, p_hi], axis=0)
@@ -332,10 +376,10 @@
     def unfold(v):
         return jnp.concatenate([v[:, :n], v[:, n:]], axis=0)
 
+    z_times_m(3)
+    tcopy[1].start()
     sum_start(0, 0, fold(quarters(mm(zz[...], zz[...], NT))))
     zcopy.start()
-    z_times_m(3)
-    tcopy[1].start()
     z_times_m(4)
     tcopy[1].wait_recv()
 
@@ -384,7 +428,7 @@
     proj[...] = mm_high(mm_high(li, sym, NN), li, NT)
     for c in ocopy:
         c.wait()
-    for c in xcopy + shared[1:2] + [zcopy] + scopy + bcopy + tcopy:
+    for c in xown + xpass + shared[1:2] + [zcopy] + scopy + bown + bpass + tcopy:
         c.wait_send()
     pl.when(h == 1)(shared[0].wait_send)
     pl.when(h == 0)(shared[2].wait_send)
@@ -400,14 +444,8 @@
     half, length = current.shape
     states = rotation.shape[1]
     total_rows = ntot // W
-    rows = lax.axis_index("row") * rows_here + jnp.arange(rows_here, dtype=jnp.int32)
-    offsets = jnp.mod(columns - rows[:, None], total_rows)
-    hit = offsets[:, None, :] == jnp.arange(WB + 1, dtype=jnp.int32)[None, :, None]
-    inv = slots + jnp.sum(jnp.where(hit, jnp.arange(slots, dtype=jnp.int32) - slots, 0), axis=2)
-
     any_ = pl.BlockSpec(memory_space=pl.ANY)
     vmem = pl.BlockSpec(memory_space=pltpu.VMEM)
-    smem = pl.BlockSpec(memory_space=pltpu.SMEM)
     ga = 2 * dims[-1]
     gb = total_rows // rows_here // dims[-1]
     dma = pltpu.SemaphoreType.DMA
@@ -428,12 +466,16 @@
         pltpu.VMEM((states, W), F32),
         pltpu.VMEM((states, 3 * states), F32),
         pltpu.VMEM((1, half), F32),
+        pltpu.VMEM((rows_here, slots), jnp.int32),
+        pltpu.VMEM((RB, W), jnp.int32),
+        pltpu.SMEM((RB, W), jnp.int32),
+        pltpu.VMEM((half, L), F32),
         pltpu.VMEM((2, states, L), F32),
         pltpu.VMEM((2, ga, half, 2 * states), F32),
         pltpu.VMEM((2, gb, half, 2 * states), F32),
-        dma((RB,)), dma((6,)), dma((3,)), dma((3,)),
-        dma((2,)), dma((2,)), dma((3,)), dma((3,)), dma(()), dma(()), dma((3,)), dma((3,)),
-        dma((SLABS,)), dma((SLABS,)),
+        dma((RB,)), dma((9,)), dma((3,)), dma((3,)),
+        dma((4,)), dma((4,)), dma((3,)), dma((3,)), dma(()), dma(()), dma((3,)), dma((3,)),
+        dma((2,)), dma((2,)), dma((4,)), dma((4,)),
         dma((2, ga)), dma((2, ga)), dma((2, gb)), dma((2, gb)), dma((2,)), dma((2,)),
     ]
     outs = pl.pallas_call(
@@ -443,14 +485,14 @@
             jax.ShapeDtypeStruct((half, length), F32),
             jax.ShapeDtypeStruct((states, states), F32),
         ),
-        in_specs=[smem, any_, any_, any_, any_, any_],
+        in_specs=[any_, any_, any_, any_, any_, any_],
         out_specs=(any_, any_, vmem),
         scratch_shapes=scratch,
         compiler_params=pltpu.CompilerParams(
             collective_id=0, has_side_effects=True, vmem_limit_bytes=58 * 2**20
         ),
         name="lobpcg",
-    )(inv, blocks, current, directions, ritz_values.reshape(1, half), rotation.T)
+    )(columns, blocks, current, directions, ritz_values.reshape(1, half), rotation.T)
     return pl.pallas_call(
         place,
         out_shape=tuple(jax.ShapeDtypeStruct(o.shape, o.dtype) for o in outs),

time: 67.6 us -> 63.8 us (0.944)
  Pallas kernels: 64.4 us -> 62.6 us
  other arithmetic: 1.54 us -> 0 us
    pallas_call x1, Pallas kernels: 62.5 us -> 60.8 us  [on_device(): pl.pallas_call(functools.partial(kernel, dims, ntot), out_shape=(jax.Shap...]
    select_n x1 -> x0, other arithmetic: 0.78 us -> none  [on_device(): offsets = jnp.mod(columns - rows[:, None], total_rows)]
where the time goes in v4:
time: 63.8 us; the launch traced here: 63.3 us
  Pallas kernels  62.6 us (98%)
  between operations  0.64 us (1%)
    pallas_call x1, Pallas kernels, on_device(): pl.pallas_call(functools.partial(kernel, dims, ntot), out_shape=(jax.Shap...  60.8 us
    pallas_call x1, Pallas kernels, on_device(): pl.pallas_call(place, out_shape=tuple((jax.ShapeDtypeStruct(o.shape, o.dt...  1.84 us

profile of v4, /device:TPU:1, one launch (start us, length us, event | category | flops | bytes accessed | tf_op | source)
XLA Modules:
  0.0 63.3 jit_solution(7264996795160056133)
XLA Ops:
  0.6 60.8 %lobpcg.1 = (f32[32,2048]{1,0:T(8,128)}, f32[32,2048]{1,0:T(8,128)}, f32[64,64]{1,0:T(8,128)}) custom-call(s32[16,25]{1,0:T(8,128)} %columns.1, f32[16,25,128,128]{3,2,1,0:T(8,128)} %blocks.1, f32[32,2048]{1,0:T(8,128)} %current.1, f32[32,2048]{1,0:T(8,128)} %directions.1, f32[1,32]{1,0:T(1,128)} %bitcast.3, f32[64,192]{1,0:T(8,128)} %bitcast.2), custom_call_target="tpu_custom_call" | custom-call | tf_op jit(solution)/shard_map/lobpcg/pallas_call | solution.py:481
  61.4 1.8 %place.1 = (f32[32,2048]{1,0:T(8,128)}, f32[32,2048]{1,0:T(8,128)}, f32[64,64]{1,0:T(8,128)}) custom-call(f32[32,2048]{1,0:T(8,128)} %get-tuple-element.6.refs_0_, f32[32,2048]{1,0:T(8,128)} %get-tuple-element.7.refs_1_, f32[64,64]{1,0:T(8,128)} %get-tuple-element.8.refs_2_), custom_call_target="tpu_custom_call" | custom-call | tf_op jit(solution)/shard_map/place/pallas_call | solution.py:496

commit v5 on v4

--- a/solution.py
+++ b/solution.py
@@ -14,21 +14,17 @@
 NN = (((1,), (0,)), ((), ()))
 NT = (((1,), (1,)), ((), ()))
 TN = (((0,), (0,)), ((), ()))
-HIGH = lax.Precision.HIGHEST
 
 RB = 8
 W = 128
 L = RB * W
 SLABS = WB // RB + 1
 CH = 256
+PIECES = 4
 
 
 def mm(a, b, dims):
     return lax.dot_general(a, b, dims, preferred_element_type=F32)
-
-
-def mm_high(a, b, dims):
-    return lax.dot_general(a, b, dims, precision=HIGH, preferred_element_type=F32)
 
 
 def split(v):
@@ -70,7 +66,7 @@
 
 def kernel(dims, ntot, columns, blocks, current, directions, ritz, rot, nc, nd, proj, *scratch):
     stages = scratch[:RB]
-    (mh, ml, xw, xx, zw, zz, zzp, part, inbuf, tb, tin, hx, pv, lam, rotv, ritzv, colv, invv, inv_ref, xo, ostage, bufa, bufb,
+    (mh, ml, xw, xx, zw, zz, zzp, part, inbuf, tb, tin, hx, pv, lam, rotv, ritzv, colv, invv, inv_ref, ostage, bufa, bufb,
      blk_sem, loc_sem, exs, exr, xs, xr, cs, cr, zs, zr, ts, tr, ss, sr, bs, br, asa, ara, asb, arb, outs, outr) = scratch[RB:]
     half, full = current.shape
     slots = blocks.shape[1]
@@ -107,12 +103,14 @@
     mine = pl.multiple_of(h * L, L)
     other = pl.multiple_of((1 - h) * L, L)
     hrows = pl.multiple_of(h * half, half)
-    loc_x = pltpu.make_async_copy(current.at[:, pl.ds(mine, L)], xw.at[h, pl.ds(hrows, half)], loc_sem.at[0])
-    loc_x.start()
+    loc_x = [
+        pltpu.make_async_copy(current.at[:, pl.ds(w * L, L)], xw.at[w, pl.ds(hrows, half)], loc_sem.at[8 * w])
+        for w in range(2)
+    ]
+    for c in loc_x:
+        c.start()
     loc_p = pltpu.make_async_copy(directions.at[:, pl.ds(mine, L)], pv.at[pl.ds(hrows, half)], loc_sem.at[1])
     loc_p.start()
-    loc_xo = pltpu.make_async_copy(current.at[:, pl.ds(other, L)], xo, loc_sem.at[8])
-    loc_xo.start()
     loc_rot = pltpu.make_async_copy(rot, rotv, loc_sem.at[4])
     loc_rot.start()
     loc_ritz = pltpu.make_async_copy(ritz, ritzv, loc_sem.at[5])
@@ -139,7 +137,8 @@
     to_smem = pltpu.make_async_copy(invv, inv_ref, loc_sem.at[7])
     to_smem.start()
     to_smem.wait()
-    loc_xo.wait()
+    for c in loc_x:
+        c.wait()
     pl.semaphore_wait(barrier, len(partners))
 
     def remote(src, dst, ssem, rsem, dev):
@@ -147,26 +146,37 @@
             src_ref=src, dst_ref=dst, send_sem=ssem, recv_sem=rsem, device_id=dev, device_id_type=MESH)
 
     ex = [
-        remote(xo, xw.at[1 - h, pl.ds(hrows, half)], exs.at[0], exr.at[0], sib),
+        remote(xw.at[1 - h, pl.ds(hrows, half)], xw.at[1 - h, pl.ds(hrows, half)], exs.at[0], exr.at[0], sib),
         remote(directions.at[:, pl.ds(other, L)], pv.at[pl.ds(hrows, half)], exs.at[1], exr.at[1], sib),
         remote(lam.at[pl.ds(hrows, half)], lam.at[pl.ds(hrows, half)], exs.at[2], exr.at[2], sib),
     ]
-    for c in ex[:2]:
-        c.start()
-    piece = [pl.ds(c * half, half) for c in range(2)]
+    ex[0].start()
+    piece = [pl.ds(c * (2 * half // PIECES), 2 * half // PIECES) for c in range(PIECES)]
 
     def pieces(src, i, dst, j, ssem, rsem, first, dev):
         return [remote(src.at[i, p], dst.at[j, p], ssem.at[first + c], rsem.at[first + c], dev) for c, p in enumerate(piece)]
 
-    xown = pieces(xw, h, xw, h + 2, xs, xr, 0, row_at(-1))
-    xpass = pieces(xw, h + 2, xw, h + 4, xs, xr, 2, row_at(-1))
-    shared = [remote(xw.at[w], xw.at[w], cs.at[k], cr.at[k], sib) for k, w in enumerate((1, 2 + h, 4))]
-    got = remote(xw.at[3 - h], xw.at[3 - h], cs.at[1], cr.at[1], sib)
+    def x_piece(c, w):
+        return xw.at[w, pl.ds(pl.multiple_of(hrows + c % 2 * (half // 2), half // 2), half // 2)]
+
+    xown = [remote(x_piece(c, c // 2), x_piece(c, c // 2 + 2), xs.at[c], xr.at[c], row_at(-1)) for c in range(PIECES)]
+    xpass = [
+        remote(x_piece(c, c // 2 + 2), x_piece(c, c // 2 + 4), xs.at[PIECES + c], xr.at[PIECES + c], row_at(-1))
+        for c in range(PIECES)
+    ]
+    shared = [
+        remote(xw.at[w, pl.ds(hrows, half)], xw.at[w, pl.ds(hrows, half)], cs.at[w - 1], cr.at[w - 1], sib)
+        for w in range(1, SLABS + 1)
+    ]
+    for c in xown:
+        c.start()
+    pl.when(h == 1)(shared[0].start)
+    ex[1].start()
     zcopy = remote(zw.at[0], zw.at[1], zs, zr, row_at(-1))
     tcopy = [remote(tb.at[t], tin.at[k], ts.at[k], tr.at[k], dev) for k, (t, dev) in enumerate(((1, sib), (3, sib), (4, row_at(1))))]
     scopy = [remote(part.at[t], inbuf.at[t], ss.at[t // 2], sr.at[t // 2], sib) for t in (1, 3)]
     bown = pieces(part, 4, inbuf, 4, bs, br, 0, row_at(1))
-    bpass = pieces(part, 2, inbuf, 2, bs, br, 2, row_at(1))
+    bpass = pieces(part, 2, inbuf, 2, bs, br, PIECES, row_at(1))
 
     def to_parts(t):
         hi, lo = split(xw[h + t])
@@ -227,21 +237,19 @@
             part[t, :, at] = v
         times_m(xx.at[0], t, put)
 
-    loc_x.wait()
-    for i in range(RB // 2):
+    for i in range(RB):
         expand(i)
     ex[0].wait()
-    for c in xown:
-        c.start()
-    pl.when(h == 1)(shared[0].start)
-    for i in range(RB // 2, RB):
-        expand(i)
     to_parts(0)
     er = lax.broadcasted_iota(jnp.int32, (half, half), 0) == lax.broadcasted_iota(jnp.int32, (half, half), 1)
     loc_ritz.wait()
     lam_own = jnp.sum(jnp.where(er, jnp.broadcast_to(ritzv[...], (half, half)), 0.0), axis=1, keepdims=True)
     lam[pl.ds(hrows, half), :] = jnp.broadcast_to(lam_own, (half, W))
     ex[2].start()
+    def pass_x(c):
+        xown[c].wait_recv()
+        xpass[c].start()
+
     back(3)
     scopy[1].start()
     back(4)
@@ -255,8 +263,9 @@
     back(1)
     scopy[0].start()
     back(2)
-    xown[0].wait_recv()
-    xpass[0].start()
+    pass_x(0)
+    pass_x(1)
+    shared[1].start()
 
     @pl.when(h == 0)
     def _():
@@ -276,27 +285,31 @@
     def put_hx(at, v):
         hx[:, at] = v
     times_m(xx.at[0], 0, put_hx)
+    pass_x(2)
+    pass_x(3)
+    shared[2].start()
     times_mt(0)
-    xown[1].wait_recv()
-    xpass[1].start()
-    shared[1].start()
-    pl.when(h == 0)(shared[0].wait_recv)
-    pl.when(h == 1)(got.wait_recv)
-    to_parts(1)
-    times_mt(1)
     pass_products(0)
-    to_parts(2)
-    times_mt(2)
+
+    def direct(t):
+        pl.when(h == 0)(shared[t - 1].wait_recv)
+        pl.when(h == 1)(shared[t].wait_recv)
+        to_parts(t)
+        times_mt(t)
+
+    direct(1)
     pass_products(1)
-    for c in xpass:
+    pass_products(2)
+    for c in xpass[:2]:
         c.wait_recv()
-    pl.when(h == 0)(shared[2].start)
-    to_parts(4)
-    times_mt(4)
-    pl.when(h == 0)(got.wait_recv)
-    pl.when(h == 1)(shared[2].wait_recv)
-    to_parts(3)
-    times_mt(3)
+    shared[3].start()
+    direct(2)
+    pass_products(3)
+    for c in xpass[2:]:
+        c.wait_recv()
+    pl.when(h == 0)(shared[4].start)
+    direct(3)
+    direct(4)
     loc_p.wait()
     ex[1].wait()
     ex[2].wait()
@@ -425,13 +438,15 @@
         c.start()
     s = unfold(sum_finish(1, 1)) * (1.0 / ntot)
     sym = s + jnp.transpose(s)
-    proj[...] = mm_high(mm_high(li, sym, NN), li, NT)
+    v = mm(ll, jnp.concatenate(split(sym), axis=0), NN)
+    v = jnp.concatenate(split(v[:n] + v[n:]), axis=0)
+    proj[...] = quarters(mm(v, jnp.concatenate([li_hi, li_lo], axis=0), NT))
     for c in ocopy:
         c.wait()
-    for c in xown + xpass + shared[1:2] + [zcopy] + scopy + bown + bpass + tcopy:
+    for c in xown + xpass + shared[1:4] + [zcopy] + scopy + bown + bpass + tcopy:
         c.wait_send()
     pl.when(h == 1)(shared[0].wait_send)
-    pl.when(h == 0)(shared[2].wait_send)
+    pl.when(h == 0)(shared[4].wait_send)
 
 
 def place(*refs):
@@ -469,13 +484,12 @@
         pltpu.VMEM((rows_here, slots), jnp.int32),
         pltpu.VMEM((RB, W), jnp.int32),
         pltpu.SMEM((RB, W), jnp.int32),
-        pltpu.VMEM((half, L), F32),
         pltpu.VMEM((2, states, L), F32),
         pltpu.VMEM((2, ga, half, 2 * states), F32),
         pltpu.VMEM((2, gb, half, 2 * states), F32),
         dma((RB,)), dma((9,)), dma((3,)), dma((3,)),
-        dma((4,)), dma((4,)), dma((3,)), dma((3,)), dma(()), dma(()), dma((3,)), dma((3,)),
-        dma((2,)), dma((2,)), dma((4,)), dma((4,)),
+        dma((2 * PIECES,)), dma((2 * PIECES,)), dma((SLABS,)), dma((SLABS,)), dma(()), dma(()), dma((3,)), dma((3,)),
+        dma((2,)), dma((2,)), dma((2 * PIECES,)), dma((2 * PIECES,)),
         dma((2, ga)), dma((2, ga)), dma((2, gb)), dma((2, gb)), dma((2,)), dma((2,)),
     ]
     outs = pl.pallas_call(

time: 63.8 us -> 62.8 us (0.984)
  Pallas kernels: 62.6 us -> 61.8 us
    pallas_call x1, Pallas kernels: 60.8 us -> 59.9 us  [on_device(): pl.pallas_call(functools.partial(kernel, dims, ntot), out_shape=(jax.Shap...]
where the time goes in v5:
time: 62.8 us; the launch traced here: 62.4 us
  Pallas kernels  61.8 us (98%)
  between operations  0.64 us (1%)
    pallas_call x1, Pallas kernels, on_device(): pl.pallas_call(functools.partial(kernel, dims, ntot), out_shape=(jax.Shap...  59.9 us
    pallas_call x1, Pallas kernels, on_device(): pl.pallas_call(place, out_shape=tuple((jax.ShapeDtypeStruct(o.shape, o.dt...  1.84 us

profile of v5, /device:TPU:1, one launch (start us, length us, event | category | flops | bytes accessed | tf_op | source)
XLA Modules:
  0.0 62.4 jit_solution(632970225327457097)
XLA Ops:
  0.6 59.9 %lobpcg.1 = (f32[32,2048]{1,0:T(8,128)}, f32[32,2048]{1,0:T(8,128)}, f32[64,64]{1,0:T(8,128)}) custom-call(s32[16,25]{1,0:T(8,128)} %columns.1, f32[16,25,128,128]{3,2,1,0:T(8,128)} %blocks.1, f32[32,2048]{1,0:T(8,128)} %current.1, f32[32,2048]{1,0:T(8,128)} %directions.1, f32[1,32]{1,0:T(1,128)} %bitcast.3, f32[64,192]{1,0:T(8,128)} %bitcast.2), custom_call_target="tpu_custom_call" | custom-call | tf_op jit(solution)/shard_map/lobpcg/pallas_call | solution.py:495
  60.6 1.8 %place.1 = (f32[32,2048]{1,0:T(8,128)}, f32[32,2048]{1,0:T(8,128)}, f32[64,64]{1,0:T(8,128)}) custom-call(f32[32,2048]{1,0:T(8,128)} %get-tuple-element.6.refs_0_, f32[32,2048]{1,0:T(8,128)} %get-tuple-element.7.refs_1_, f32[64,64]{1,0:T(8,128)} %get-tuple-element.8.refs_2_), custom_call_target="tpu_custom_call" | custom-call | tf_op jit(solution)/shard_map/place/pallas_call | solution.py:510

commit v6 on v5

--- a/solution.py
+++ b/solution.py
@@ -289,7 +289,6 @@
     pass_x(3)
     shared[2].start()
     times_mt(0)
-    pass_products(0)
 
     def direct(t):
         pl.when(h == 0)(shared[t - 1].wait_recv)
@@ -298,12 +297,13 @@
         times_mt(t)
 
     direct(1)
+    pass_products(0)
     pass_products(1)
-    pass_products(2)
     for c in xpass[:2]:
         c.wait_recv()
     shared[3].start()
     direct(2)
+    pass_products(2)
     pass_products(3)
     for c in xpass[2:]:
         c.wait_recv()
@@ -417,10 +417,9 @@
     tb[2] += tin[2]
     s = s + s_part(1)
     sum_start(1, 0, fold(quarters(s)))
+    sum_start(1, 1, sum_finish(1, 0))
     a = factor_start(unfold(sum_finish(0, 1)) * (1.0 / ntot))
-    a = factor_steps(a, 0, half)
-    sum_start(1, 1, sum_finish(1, 0))
-    a = factor_steps(a, half, n)
+    a = factor_steps(a, 0, n)
     li = factor_end(a)
     li_hi, li_lo = split(li)
     ll = jnp.concatenate([jnp.concatenate([li_hi, li_hi], axis=1), jnp.concatenate([li_lo, li_lo], axis=1)], axis=0)

time: 62.8 us -> 60.8 us (0.968)
  Pallas kernels: 61.8 us -> 60.1 us
    pallas_call x1, Pallas kernels: 59.9 us -> 58.2 us  [on_device(): pl.pallas_call(functools.partial(kernel, dims, ntot), out_shape=(jax.Shap...]
where the time goes in v6:
time: 60.8 us; the launch traced here: 60.7 us
  Pallas kernels  60.1 us (99%)
  between operations  0.64 us (1%)
    pallas_call x1, Pallas kernels, on_device(): pl.pallas_call(functools.partial(kernel, dims, ntot), out_shape=(jax.Shap...  58.2 us
    pallas_call x1, Pallas kernels, on_device(): pl.pallas_call(place, out_shape=tuple((jax.ShapeDtypeStruct(o.shape, o.dt...  1.84 us

profile of v6, /device:TPU:1, one launch (start us, length us, event | category | flops | bytes accessed | tf_op | source)
XLA Modules:
  0.0 60.7 jit_solution(10368335317302027396)
XLA Ops:
  0.6 58.2 %lobpcg.1 = (f32[32,2048]{1,0:T(8,128)}, f32[32,2048]{1,0:T(8,128)}, f32[64,64]{1,0:T(8,128)}) custom-call(s32[16,25]{1,0:T(8,128)} %columns.1, f32[16,25,128,128]{3,2,1,0:T(8,128)} %blocks.1, f32[32,2048]{1,0:T(8,128)} %current.1, f32[32,2048]{1,0:T(8,128)} %directions.1, f32[1,32]{1,0:T(1,128)} %bitcast.3, f32[64,192]{1,0:T(8,128)} %bitcast.2), custom_call_target="tpu_custom_call" | custom-call | tf_op jit(solution)/shard_map/lobpcg/pallas_call | solution.py:494
  58.9 1.8 %place.1 = (f32[32,2048]{1,0:T(8,128)}, f32[32,2048]{1,0:T(8,128)}, f32[64,64]{1,0:T(8,128)}) custom-call(f32[32,2048]{1,0:T(8,128)} %get-tuple-element.6.refs_0_, f32[32,2048]{1,0:T(8,128)} %get-tuple-element.7.refs_1_, f32[64,64]{1,0:T(8,128)} %get-tuple-element.8.refs_2_), custom_call_target="tpu_custom_call" | custom-call | tf_op jit(solution)/shard_map/place/pallas_call | solution.py:509

commit v7 on v6

--- a/solution.py
+++ b/solution.py
@@ -66,7 +66,7 @@
 
 def kernel(dims, ntot, columns, blocks, current, directions, ritz, rot, nc, nd, proj, *scratch):
     stages = scratch[:RB]
-    (mh, ml, xw, xx, zw, zz, zzp, part, inbuf, tb, tin, hx, pv, lam, rotv, ritzv, colv, invv, inv_ref, ostage, bufa, bufb,
+    (mh, ml, xw, xx, zw, zz, zzp, part, inbuf, tb, tin, hx, hxt, pv, lam, rotv, ritzv, colv, invv, inv_ref, ostage, bufa, bufb,
      blk_sem, loc_sem, exs, exr, xs, xr, cs, cr, zs, zr, ts, tr, ss, sr, bs, br, asa, ara, asb, arb, outs, outr) = scratch[RB:]
     half, full = current.shape
     slots = blocks.shape[1]
@@ -219,9 +219,9 @@
     def times_mt(t):
         def chunk(j, lo, hi):
             at = pl.ds(pl.multiple_of(j * CH, CH), CH)
-            a = mm(xx[t, :, lo:hi], mh[at, t * L + lo:t * L + hi], NT)
-            b = mm(xx[t, :2 * half, lo:hi], ml[at, t * L + lo:t * L + hi], NT)
-            hx[:, at] += a[:2 * half] + a[2 * half:] + b
+            v = mm(mh[at, t * L + lo:t * L + hi], xx[t, :, lo:hi], NT)
+            v = v + mm(ml[at, t * L + lo:t * L + hi], xx[t, :, lo:hi], NT)
+            hxt[at, :] = v if t == 0 else hxt[at, :] + v
 
         if t == 0 or t == SLABS - 1:
             for j in range(L // CH):
@@ -328,7 +328,8 @@
     for j in range(L // CH):
         at = slice(j * CH, (j + 1) * CH)
         x = xw[h, :, at]
-        res = hx[:, at] + inbuf[2, :, at] - jnp.concatenate([lam[...]] * (CH // W), axis=1) * x
+        cols = jnp.transpose(hxt[at, :])
+        res = cols[:n] + cols[n:] + hx[:, at] + inbuf[2, :, at] - jnp.concatenate([lam[...]] * (CH // W), axis=1) * x
         r_hi, r_lo = split(res)
         p_hi, p_lo = split(pv[:, at])
         b_hi = jnp.concatenate([xx[0, :n, at], r_hi, p_hi], axis=0)
@@ -476,6 +477,7 @@
         pltpu.VMEM((SLABS, states, L), F32),
         pltpu.VMEM((3, states, L), F32),
         pltpu.VMEM((states, L), F32),
+        pltpu.VMEM((L, 2 * states), F32),
         pltpu.VMEM((states, L), F32),
         pltpu.VMEM((states, W), F32),
         pltpu.VMEM((states, 3 * states), F32),

time: 60.8 us -> 60.9 us (level)
  no operation moved by 1% of the time
where the time goes in v7:
time: 60.9 us; the launch traced here: 60.8 us
  Pallas kernels  60.1 us (99%)
  between operations  0.64 us (1%)
    pallas_call x1, Pallas kernels, on_device(): pl.pallas_call(functools.partial(kernel, dims, ntot), out_shape=(jax.Shap...  58.3 us
    pallas_call x1, Pallas kernels, on_device(): pl.pallas_call(place, out_shape=tuple((jax.ShapeDtypeStruct(o.shape, o.dt...  1.84 us

profile of v7, /device:TPU:1, one launch (start us, length us, event | category | flops | bytes accessed | tf_op | source)
XLA Modules:
  0.0 60.8 jit_solution(3924592510772649837)
XLA Ops:
  0.6 58.3 %lobpcg.1 = (f32[32,2048]{1,0:T(8,128)}, f32[32,2048]{1,0:T(8,128)}, f32[64,64]{1,0:T(8,128)}) custom-call(s32[16,25]{1,0:T(8,128)} %columns.1, f32[16,25,128,128]{3,2,1,0:T(8,128)} %blocks.1, f32[32,2048]{1,0:T(8,128)} %current.1, f32[32,2048]{1,0:T(8,128)} %directions.1, f32[1,32]{1,0:T(1,128)} %bitcast.3, f32[64,192]{1,0:T(8,128)} %bitcast.2), custom_call_target="tpu_custom_call" | custom-call | tf_op jit(solution)/shard_map/lobpcg/pallas_call | solution.py:496
  58.9 1.8 %place.1 = (f32[32,2048]{1,0:T(8,128)}, f32[32,2048]{1,0:T(8,128)}, f32[64,64]{1,0:T(8,128)}) custom-call(f32[32,2048]{1,0:T(8,128)} %get-tuple-element.6.refs_0_, f32[32,2048]{1,0:T(8,128)} %get-tuple-element.7.refs_1_, f32[64,64]{1,0:T(8,128)} %get-tuple-element.8.refs_2_), custom_call_target="tpu_custom_call" | custom-call | tf_op jit(solution)/shard_map/place/pallas_call | solution.py:511
